TPU v7x, 32 devices: a whole 2x2x4 slice. The times are simulated.
32 devices in a mesh: space: 4 (over y, x), dp: 8 (over z, core).
Axes of the slice: x: 2, y: 2, z: 4, core: 2. Of those that a mesh axis runs over, the one named last changes fastest.
Arguments:
- volumes: bfloat16 [8, 4, 32, 8, 128], P('dp', None, 'space'), may hold values from -6 to 6
- first_kernel: bfloat16 [16, 4, 3, 3, 3], replicated, may hold values from -1 to 1
- middle_kernel: bfloat16 [32, 16, 3, 3, 3], replicated, may hold values from -0.5 to 0.5
- cotangent: bfloat16 [8, 32, 8, 2, 32], P('dp', None, 'space'), may hold values from -48 to 48
Outputs:
- features: bfloat16 [8, 32, 8, 2, 32], P('dp', None, 'space')
- first_grad: float32 [16, 4, 3, 3, 3], replicated
- middle_grad: float32 [32, 16, 3, 3, 3], replicated
All inputs are finite; a program needn't handle non-finite values.
Results may differ from a plain program's by a relative error of at most 0.007.
Values may be sent and summed in bfloat16 or wider, within the bound.
A program may use at most 64 MiB of HBM per device.

v0:
```python
import functools
import math

import jax
import jax.numpy as jnp
from jax import lax
from jax.experimental import pallas as pl
from jax.experimental.pallas import tpu as pltpu
from jax.sharding import PartitionSpec as P

leak_slope = 0.3
soft_share = 0.7
log_two = math.log(2.0)
reach = 5
f32, bf16 = jnp.float32, jnp.bfloat16


def activate(a):
    soft = jnp.maximum(a, 0.0) + jnp.log(1.0 + jnp.exp(-jnp.abs(a)))
    return leak_slope * a + soft_share * (soft - log_two)


def slope_of(a):
    return leak_slope + soft_share / (1.0 + jnp.exp(-a))


def dot(a, b):
    return jnp.dot(a, b, preferred_element_type=f32)


def dot_lanes(a, b):
    return lax.dot_general(a, b, (((1,), (1,)), ((), ())), preferred_element_type=f32)


def dot_wide(a, b):
    high = a.astype(bf16)
    low = (a - high.astype(f32)).astype(bf16)
    return dot(high, b) + dot(low, b)


def grid_of(rows, cols):
    return (
        lax.broadcasted_iota(jnp.int32, (rows, cols), 0),
        lax.broadcasted_iota(jnp.int32, (rows, cols), 1),
    )


def pick(where, value=1.0):
    return jnp.where(where, value, 0.0).astype(bf16)


def z_taps(a, width):
    place = lax.broadcasted_iota(jnp.int32, a.shape, 1) & (width - 1)
    before = jnp.where(place == 0, 0.0, pltpu.roll(a, 1, 1))
    after = jnp.where(place == width - 1, 0.0, pltpu.roll(a, 127, 1))
    return jnp.concatenate([before, a, after], axis=0).astype(bf16)


def between(a, b):
    place = lax.broadcasted_iota(jnp.int32, a.shape, 1)
    return jnp.where(place < 64, pltpu.roll(a, 64, 1), pltpu.roll(b, 64, 1))


def kernel(
    n_space, n_dp, part,
    vol_ref, w1_ref, w2_ref, cot_ref,
    feat_ref, g1_ref, g2_ref,
    vol_left, vol_right, cot_left, cot_right, pay, got, across, full,
    halo_send, halo_recv, rs_send, rs_recv, ex_send, ex_recv, ag_send, ag_recv,
):
    s, d = lax.axis_index("space"), lax.axis_index("dp")
    n_a, n_b = 2 * n_space, n_dp // 2
    a, b = 2 * s + lax.rem(d, 2), d // 2
    inner = s > 0
    outer = s < n_space - 1

    def in_a(step):
        t = lax.rem(a + step, n_a)
        return t, {"space": t // 2, "dp": 2 * b + lax.rem(t, 2)}

    def in_b(step):
        t = lax.rem(b + step, n_b)
        return t, {"space": s, "dp": 2 * t + lax.rem(d, 2)}

    for ref in (vol_left, vol_right, cot_left, cot_right):
        ref[...] = jnp.zeros_like(ref)
    barrier = pltpu.get_barrier_semaphore()
    for step in range(1, n_a):
        pl.semaphore_signal(barrier, inc=1, device_id=in_a(step)[1], device_id_type=pl.DeviceIdType.MESH)
    for step in range(1, n_b):
        pl.semaphore_signal(barrier, inc=1, device_id=in_b(step)[1], device_id_type=pl.DeviceIdType.MESH)

    lane = lax.broadcasted_iota(jnp.int32, (1, 128), 1)
    deep_y = 2 * (lane & 1) + (lane >> 6)
    ro, co = grid_of(32, 128)
    t2 = dot(w2_ref[...].reshape(27 * 16, 32), pick(ro == (co & 63) >> 1))
    ro, co = grid_of(16, 128)
    w1 = jnp.concatenate([w1_ref[k].astype(f32) for k in range(27)], axis=0).astype(bf16)
    t1 = dot(w1, pick(ro == (co & 15)))
    ro, co = grid_of(8, 128)
    near_y = 2 * ((co & 63) >> 4) + (co >> 6)
    taps_y = [jnp.where(ro == near_y + q - 1, 1.0, 0.0) for q in range(3)]

    def tap2(k):
        return t2[16 * k : 16 * k + 16]

    w1_rows, w2_rows, wb_cols = [], [], []
    for p in range(3):
        for r in range(3):
            for c in range(4):
                rows = [4 * (9 * p + 3 * q + r) + c for q in range(3)]
                w1_rows.append(sum(t1[k : k + 1] * taps_y[q] for q, k in enumerate(rows)))
            ks = [9 * p + 3 * q + r for q in range(3)]
            block = []
            for y in range(4):
                w2_rows.append(sum(jnp.where(deep_y == y + 1 - q, tap2(k), 0.0) for q, k in enumerate(ks)))
                block.append(sum(jnp.where(deep_y == y + q - 1, tap2(26 - k), 0.0) for q, k in enumerate(ks)))
            wb_cols.append(jnp.concatenate(block, axis=0))
    w1_wide = jnp.concatenate(w1_rows, axis=0).T.astype(bf16)
    w2_wide = jnp.concatenate(w2_rows, axis=0).T.astype(bf16)
    wb_wide = jnp.concatenate(wb_cols, axis=1).astype(bf16)

    pl.semaphore_wait(barrier, n_a - 1 + n_b - 1)
    right = {"space": jnp.minimum(s + 1, n_space - 1), "dp": d}
    left = {"space": jnp.maximum(s - 1, 0), "dp": d}

    def halo(src, dst, sem, to):
        return pltpu.make_async_remote_copy(
            src_ref=src, dst_ref=dst, send_sem=halo_send.at[sem], recv_sem=halo_recv.at[sem],
            device_id=to, device_id_type=pl.DeviceIdType.MESH,
        )

    size_x = vol_ref.shape[1]
    to_right = [halo(vol_ref.at[:, size_x - reach : size_x], vol_left, 0, right), halo(cot_ref, cot_left, 1, right)]
    to_left = [halo(vol_ref.at[:, 0:reach], vol_right, 2, left), halo(cot_ref, cot_right, 3, left)]

    @pl.when(outer)
    def _():
        for copy in to_right:
            copy.start()

    @pl.when(inner)
    def _():
        for copy in to_left:
            copy.start()

    @pl.when(outer)
    def _():
        for copy in to_right:
            copy.wait_send()
        for copy in to_left:
            copy.wait_recv()

    @pl.when(inner)
    def _():
        for copy in to_left:
            copy.wait_send()
        for copy in to_right:
            copy.wait_recv()

    slabs = [(vol_left, i) for i in range(reach)] + [(vol_ref, i) for i in range(size_x)]
    slabs += [(vol_right, i) for i in range(reach)]
    taps = [z_taps(ref[:, i].astype(f32).reshape(32, 128), 128) for ref, i in slabs]
    taps = jnp.concatenate(taps, axis=1)
    count = 128 * (len(slabs) - 2)
    cols1 = jnp.concatenate([taps[:, 128 * p : 128 * p + count] for p in range(3)], axis=0)
    pre1 = dot(w1_wide, cols1)
    act1 = activate(pre1)
    act1 = act1[:64] + act1[64:]
    pairs = []
    for j in range(4):
        four = [act1[:, 128 * (4 * j + i) : 128 * (4 * j + i + 1)] for i in range(4)]
        pairs.append(jnp.concatenate([four[0] + four[1], four[2] + four[3]], axis=1))
    ro, co = grid_of(256, 128)
    pool = pick((ro >> 7 == co >> 6) & ((ro & 127) >> 1 == (co & 63)), 0.125)
    acts = dot_wide(jnp.concatenate(pairs, axis=0), pool).astype(bf16).astype(f32)
    even = [acts[64 * j : 64 * j + 64] for j in range(4)]
    even[0] = jnp.where(inner, even[0], 0.0)
    even[3] = jnp.where(outer, even[3], 0.0)
    odd = [between(even[j], even[j + 1]) for j in range(3)]

    even_taps = [z_taps(x, 64) for x in even]
    odd_taps = [z_taps(x, 64) for x in odd]
    cols2 = jnp.concatenate(
        [jnp.concatenate([even_taps[j], odd_taps[j], even_taps[j + 1]], axis=0) for j in range(3)], axis=1
    )
    pre2 = dot(w2_wide, cols2)
    act2 = activate(pre2)
    ro, co = grid_of(384, 64)
    row = ro >> 6
    pool = (row >= 1) & (row <= 4) & ((row - 1) >> 1 == co >> 5) & ((ro & 63) >> 1 == (co & 31))
    feat_ref[...] = dot_wide(act2[:64] + act2[64:], pick(pool, 0.125)).astype(bf16)

    ro, co = grid_of(64, 384)
    row = co >> 6
    same = (ro & 31) == (co & 63) >> 1
    wide = dot(cot_ref[...], pick(same & (row >= 1) & (row <= 4) & ((row - 1) >> 1 == ro >> 5), 0.125))
    wide += dot(cot_left[...], pick(same & (row == 0) & (ro >> 5 == 1), 0.125))
    wide += dot(cot_right[...], pick(same & (row == 5) & (ro >> 5 == 0), 0.125))
    delta2 = (slope_of(pre2) * jnp.concatenate([wide, wide], axis=0)).astype(bf16).astype(f32)
    row = lax.broadcasted_iota(jnp.int32, (128, 384), 1) >> 6
    own2 = jnp.where((row >= 1) & (row <= 4), delta2, 0.0).astype(bf16)

    odd = [delta2[:, 128 * j : 128 * j + 128] for j in range(3)]
    odd_taps = [z_taps(x, 64) for x in odd]
    even_taps = [z_taps(between(odd[j], odd[j + 1]), 64) for j in range(2)]
    cols3 = jnp.concatenate(
        [jnp.concatenate([odd_taps[j], even_taps[j], odd_taps[j + 1]], axis=0) for j in range(2)], axis=1
    )
    back = dot(wb_wide, cols3).astype(bf16)
    ro, co = grid_of(128, 256)
    spread = pick((ro >> 6 == co >> 7) & ((ro & 63) == (co & 127) >> 1), 0.125)
    wide = dot(jnp.concatenate([back[:, :128], back[:, 128:]], axis=0), spread)
    rows = [wide[64 * (i // 2) : 64 * (i // 2) + 64, 128 * (i % 2) : 128 * (i % 2) + 128] for i in range(4)]
    wide = jnp.concatenate([rows[i // 2] for i in range(8)], axis=1)
    first = 128 * (reach - 1)
    own = slice(first, first + 128 * size_x)
    delta1 = (slope_of(pre1[:, own]) * jnp.concatenate([wide, wide], axis=0)).astype(bf16)

    grad2 = dot_lanes(cols2, own2)
    blocks = []
    for k in range(27):
        p, q, r = k // 9, k // 3 % 3, k % 3
        at = 64 * (3 * p + r)
        blocks.append(
            sum(jnp.where(deep_y == y + 1 - q, grad2[at + 16 * y : at + 16 * y + 16], 0.0) for y in range(4))
        )
    blocks.append(jnp.zeros((16, 128), f32))
    groups = [jnp.concatenate(blocks[7 * j : 7 * j + 7], axis=0) for j in range(4)]
    ro, co = grid_of(512, 128)
    gather = pick((ro >> 7 == co >> 5) & ((ro & 63) >> 1 == (co & 31)))
    pay[0:112] = dot_wide(jnp.concatenate(groups, axis=1), gather)

    grad1 = dot_lanes(cols1[:, own], delta1).reshape(36, 8, 128)
    groups = [jnp.sum(grad1 * taps_y[q][None], axis=1) for q in range(3)]
    groups = jnp.concatenate([jnp.concatenate(groups, axis=1), jnp.zeros((4, 384), f32)], axis=0)
    ro, co = grid_of(384, 128)
    gather = pick((ro >> 7 == co >> 4) & ((ro & 15) == (co & 15)))
    pay[112:152] = dot_wide(groups, gather)
    if n_a * part > 152:
        pay[152:] = jnp.zeros((n_a * part - 152, 128), f32)

    def rows_of(t):
        return pl.ds(pl.multiple_of(t * part, 8), part)

    copies = []
    for step in range(1, n_a):
        t, to = in_a(step)
        copies.append(pltpu.make_async_remote_copy(
            src_ref=pay.at[rows_of(t)], dst_ref=got.at[step - 1],
            send_sem=rs_send.at[step - 1], recv_sem=rs_recv.at[step - 1],
            device_id=to, device_id_type=pl.DeviceIdType.MESH,
        ))
        copies[-1].start()
    total = pay[rows_of(a)]
    for i, copy in enumerate(copies):
        copy.wait_recv()
        total += got[i]
    for copy in copies:
        copy.wait_send()

    across[b] = total
    copies = []
    for step in range(1, n_b):
        t, to = in_b(step)
        copies.append(pltpu.make_async_remote_copy(
            src_ref=across.at[b], dst_ref=across.at[b],
            send_sem=ex_send.at[step - 1], recv_sem=ex_recv.at[step - 1],
            device_id=to, device_id_type=pl.DeviceIdType.MESH,
        ))
        copies[-1].start()
    for copy in copies:
        copy.wait()
    total = across[0]
    for i in range(1, n_b):
        total += across[i]

    full[rows_of(a)] = total * (1.0 / n_dp)
    copies = []
    for step in range(1, n_a):
        t, to = in_a(step)
        copies.append(pltpu.make_async_remote_copy(
            src_ref=full.at[rows_of(a)], dst_ref=full.at[rows_of(a)],
            send_sem=ag_send.at[step - 1], recv_sem=ag_recv.at[step - 1],
            device_id=to, device_id_type=pl.DeviceIdType.MESH,
        ))
        copies[-1].start()
    for copy in copies:
        copy.wait()

    for j in range(4):
        many = 7 if j < 3 else 6
        g2_ref[7 * j : 7 * j + many] = full[0 : 16 * many, 32 * j : 32 * j + 32].reshape(many, 16, 32)
    for k in range(27):
        p, q, r = k // 9, k // 3 % 3, k % 3
        at = 112 + 4 * (3 * p + r)
        g1_ref[k] = full[at : at + 4, 16 * q : 16 * q + 16]


def shards(n_space, n_dp, volumes, first_kernel, middle_kernel, cotangent):
    n_a, n_b = 2 * n_space, n_dp // 2
    part = 8 * -(-152 // (8 * n_a))
    w1 = first_kernel.transpose(2, 3, 4, 1, 0).reshape(27, 4, 16)
    w2 = middle_kernel.transpose(2, 3, 4, 1, 0).reshape(27, 16, 32)
    cot = cotangent[0].transpose(0, 2, 1, 3).reshape(64, 64)
    vol = volumes[0]
    halo = (vol.shape[0], reach) + vol.shape[2:]
    vmem = pl.BlockSpec(memory_space=pltpu.VMEM)
    dma = pltpu.SemaphoreType.DMA
    feat, g1, g2 = pl.pallas_call(
        functools.partial(kernel, n_space, n_dp, part),
        out_shape=(
            jax.ShapeDtypeStruct((64, 64), bf16),
            jax.ShapeDtypeStruct((27, 4, 16), f32),
            jax.ShapeDtypeStruct((27, 16, 32), f32),
        ),
        in_specs=[vmem] * 4,
        out_specs=(vmem, vmem, vmem),
        scratch_shapes=[
            pltpu.VMEM(halo, bf16),
            pltpu.VMEM(halo, bf16),
            pltpu.VMEM((64, 64), bf16),
            pltpu.VMEM((64, 64), bf16),
            pltpu.VMEM((n_a * part, 128), f32),
            pltpu.VMEM((n_a - 1, part, 128), f32),
            pltpu.VMEM((n_b, part, 128), f32),
            pltpu.VMEM((n_a * part, 128), f32),
            dma((4,)), dma((4,)),
            dma((n_a - 1,)), dma((n_a - 1,)),
            dma((max(n_b - 1, 1),)), dma((max(n_b - 1, 1),)),
            dma((n_a - 1,)), dma((n_a - 1,)),
        ],
        compiler_params=pltpu.CompilerParams(
            collective_id=0, has_side_effects=True, vmem_limit_bytes=48 * 1024 * 1024
        ),
        cost_estimate=pl.CostEstimate(flops=400_000_000, bytes_accessed=400_000, transcendentals=1_000_000),
    )(vol, w1, w2, cot)
    features = feat.reshape(32, 2, 2, 32).transpose(0, 2, 1, 3)[None]
    first_grad = g1.reshape(3, 3, 3, 4, 16).transpose(4, 3, 0, 1, 2)
    middle_grad = g2.reshape(3, 3, 3, 16, 32).transpose(4, 3, 0, 1, 2)
    return (features, first_grad, middle_grad)


def solution(mesh):
    in_specs = (P("dp", None, "space", None, None), P(), P(), P("dp", None, "space", None, None))
    out_specs = (P("dp", None, "space", None, None), P(), P())
    body = functools.partial(shards, mesh.shape["space"], mesh.shape["dp"])
    return jax.shard_map(body, mesh=mesh, in_specs=in_specs, out_specs=out_specs, check_vma=False)
```

profile of v0, /device:TPU:0, one launch (start us, length us, event | category | flops | bytes accessed | tf_op | source)
XLA Modules:
  0.0 28.7 jit_solution(16106509434648123148)
XLA Ops:
  0.6 0.0 copy-start
  0.6 0.8 %copy.7 = bf16[32,2,2,32]{3,2,1,0:T(2,128)(2,1)S(1)} copy(bf16[32,2,2,32]{3,1,2,0:T(2,128)(2,1)} %bitcast.26) | data formatting | bytes 16384 | tf_op jit(solution)/shard_map/transpose | solution.py:305
  1.5 0.1 reshape.26.cot_ref
  1.5 0.0 copy-done
  1.6 0.0 copy-start.1
  1.6 0.8 %copy-done.1 = bf16[1,4,8,8,128]{4,3,2,1,0:T(8,128)(2,1)S(1)} copy-done((bf16[1,4,8,8,128]{4,3,2,1,0:T(8,128)(2,1)S(1)}, bf16[1,4,8,8,128]{4,3,2,1,0:T(8,128)(2,1)}, u32[]{:S(2)}) %copy-start.1) | copy-done | bytes 65560
  2.4 0.0 copy-start.2
  2.4 0.7 %copy-done.2 = bf16[16,4,3,3,3]{0,1,4,3,2:T(4,128)(2,1)S(1)} copy-done((bf16[16,4,3,3,3]{0,1,4,3,2:T(4,128)(2,1)S(1)}, bf16[16,4,3,3,3]{0,1,4,3,2:T(4,128)(2,1)}, u32[]{:S(2)}) %copy-start.2) | copy-done | bytes 3480
  3.1 23.6 %shard_map.67 = (bf16[64,64]{1,0:T(8,128)(2,1)S(1)}, f32[27,4,16]{2,1,0:T(4,128)S(1)}, f32[27,16,32]{2,1,0:T(8,128)S(1)}) custom-call(bf16[4,8,8,128]{3,2,1,0:T(8,128)(2,1)S(1)} %bitcast.24, bf16[27,4,16]{2,1,0:T(4,128)(2,1)S(1)} %bitcast.25, bf16[27,16,32]{2,1,0:T(8,128)(2,1)S(1)} %bitcast.23, bf16[64,64]{1,0:T(8,128)(2,1)S(1)} %reshape.26.cot_ref), custom_call_target="tpu_custom_call" | custom-call | flops 400000000 | bytes 400000 | tf_op jit(solution)/shard_map/pallas_call | solution.py:310
  26.7 0.1 reshape.27
  26.8 0.6 %copy.10 = bf16[32,2,2,32]{3,1,2,0:T(2,128)(2,1)} copy(bf16[32,2,2,32]{3,2,1,0:T(2,128)(2,1)S(1)} %reshape.27) | data formatting | bytes 16384 | tf_op jit(solution)/shard_map/reshape | solution.py:338
  27.4 0.6 %copy.13 = f32[16,4,3,3,3]{0,1,4,3,2:T(4,128)} copy(f32[16,4,3,3,3]{0,1,4,3,2:T(4,128)S(1)} %bitcast.22) | data formatting | bytes 13824
  28.1 0.7 %copy.14 = f32[32,16,3,3,3]{0,1,4,3,2:T(8,128)} copy(f32[32,16,3,3,3]{0,1,4,3,2:T(8,128)S(1)} %bitcast.21) | data formatting | bytes 110592
Async XLA Ops:
  0.6 0.9 %copy-start = (bf16[32,16,3,3,3]{0,1,4,3,2:T(8,128)(2,1)S(1)}, bf16[32,16,3,3,3]{0,1,4,3,2:T(8,128)(2,1)}, u32[]{:S(2)}) copy-start(bf16[32,16,3,3,3]{0,1,4,3,2:T(8,128)(2,1)} %param.6) | copy-start | bytes 82948
  1.6 0.8 %copy-start.1 = (bf16[1,4,8,8,128]{4,3,2,1,0:T(8,128)(2,1)S(1)}, bf16[1,4,8,8,128]{4,3,2,1,0:T(8,128)(2,1)}, u32[]{:S(2)}) copy-start(bf16[1,4,8,8,128]{4,3,2,1,0:T(8,128)(2,1)} %param.4) | copy-start | bytes 196612
  2.4 0.7 %copy-start.2 = (bf16[16,4,3,3,3]{0,1,4,3,2:T(4,128)(2,1)S(1)}, bf16[16,4,3,3,3]{0,1,4,3,2:T(4,128)(2,1)}, u32[]{:S(2)}) copy-start(bf16[16,4,3,3,3]{0,1,4,3,2:T(4,128)(2,1)} %param.5) | copy-start | bytes 10372
where the time goes:
time: 29 us; the launch traced here: 28.7 us
  Pallas kernels  23.6 us (81%)
  local copies, waits for them, and re-layouts  4.51 us (16%)
  between operations  0.67 us (2%)
    pallas_call x1, Pallas kernels, shards(): pl.pallas_call(functools.partial(kernel, n_space, n_dp, part), out_shape=...  23.6 us
    unnamed x8, local copies, waits for them, and re-layouts  2.89 us
    transpose x1, local copies, waits for them, and re-layouts, shards(): cot = cotangent[0].transpose(0, 2, 1, 3).reshape(64, 64)  0.81 us
    reshape x2, local copies, waits for them, and re-layouts, shards(): features = feat.reshape(32, 2, 2, 32).transpose(0, 2, 1, 3)[None]  0.72 us

commit v1 on v0

v1 whole, which is shorter than its diff:
```python
import functools
import math

import jax
import jax.numpy as jnp
from jax import lax
from jax.experimental import pallas as pl
from jax.experimental.pallas import tpu as pltpu
from jax.sharding import PartitionSpec as P

leak_slope = 0.3
soft_share = 0.7
log_two = math.log(2.0)
reach = 5
f32, bf16 = jnp.float32, jnp.bfloat16


def activate(a):
    soft = jnp.maximum(a, 0.0) + jnp.log(1.0 + jnp.exp(-jnp.abs(a)))
    return leak_slope * a + soft_share * (soft - log_two)


def activate_both(a):
    small = jnp.exp(-jnp.abs(a))
    whole = 1.0 + small
    soft = jnp.maximum(a, 0.0) + jnp.log(whole)
    act = leak_slope * a + soft_share * (soft - log_two)
    return act, leak_slope + soft_share * (jnp.where(a >= 0.0, 1.0, small) / whole)


def dot(a, b):
    return jnp.dot(a, b, preferred_element_type=f32)


def dot_lanes(a, b):
    return lax.dot_general(a, b, (((1,), (1,)), ((), ())), preferred_element_type=f32)


def dot_wide(a, b):
    high = a.astype(bf16)
    low = (a - high.astype(f32)).astype(bf16)
    return dot(high, b) + dot(low, b)


def grid_of(rows, cols):
    return (
        lax.broadcasted_iota(jnp.int32, (rows, cols), 0),
        lax.broadcasted_iota(jnp.int32, (rows, cols), 1),
    )


def pick(where, value=1.0):
    return jnp.where(where, value, 0.0).astype(bf16)


def z_taps(a, width):
    place = lax.broadcasted_iota(jnp.int32, a.shape, 1) & (width - 1)
    before = jnp.where(place == 0, 0.0, pltpu.roll(a, 1, 1))
    after = jnp.where(place == width - 1, 0.0, pltpu.roll(a, 127, 1))
    return jnp.concatenate([before, a, after], axis=0).astype(bf16)


def between(a, b):
    place = lax.broadcasted_iota(jnp.int32, a.shape, 1)
    return jnp.where(place < 64, pltpu.roll(a, 64, 1), pltpu.roll(b, 64, 1))


def remote(src, dst, send, recv, to):
    return pltpu.make_async_remote_copy(
        src_ref=src, dst_ref=dst, send_sem=send, recv_sem=recv, device_id=to, device_id_type=pl.DeviceIdType.MESH
    )


def kernel(
    n_space, n_dp, part,
    vol_hbm, w1_hbm, w2_hbm, cot_hbm,
    feat_ref, sums_ref,
    vol_ref, w1_ref, w2_ref, cot_ref, vol_left, vol_right, cot_left, cot_right, pay, got, across, full,
    pool1, pool2, spread1, spread2, gather1, gather2,
    load, halo_send, halo_recv, rs_send, rs_recv, ex_send, ex_recv, ag_send, ag_recv,
):
    s, d = lax.axis_index("space"), lax.axis_index("dp")
    n_a, n_b = 2 * n_space, n_dp // 2
    a, b = 2 * s + lax.rem(d, 2), d // 2
    inner = s > 0
    outer = s < n_space - 1

    def in_a(step):
        t = lax.rem(a + step, n_a)
        return t, {"space": t // 2, "dp": 2 * b + lax.rem(t, 2)}

    def in_b(step):
        t = lax.rem(b + step, n_b)
        return t, {"space": s, "dp": 2 * t + lax.rem(d, 2)}

    loads = [
        pltpu.make_async_copy(src, dst, load.at[i])
        for i, (src, dst) in enumerate(
            [(w2_hbm, w2_ref), (w1_hbm, w1_ref), (vol_hbm, vol_ref), (cot_hbm, cot_ref)]
        )
    ]
    for copy in loads:
        copy.start()
    for ref in (vol_left, vol_right, cot_left, cot_right):
        ref[...] = jnp.zeros_like(ref)
    barrier = pltpu.get_barrier_semaphore()
    for step in range(1, n_a):
        pl.semaphore_signal(barrier, inc=1, device_id=in_a(step)[1], device_id_type=pl.DeviceIdType.MESH)
    for step in range(1, n_b):
        pl.semaphore_signal(barrier, inc=1, device_id=in_b(step)[1], device_id_type=pl.DeviceIdType.MESH)
    pl.semaphore_wait(barrier, n_a - 1 + n_b - 1)

    right = {"space": jnp.minimum(s + 1, n_space - 1), "dp": d}
    left = {"space": jnp.maximum(s - 1, 0), "dp": d}
    size_x = vol_hbm.shape[1]
    deep_x = cot_hbm.shape[1]

    def halo(src, dst, sem, to):
        return remote(src, dst, halo_send.at[sem], halo_recv.at[sem], to)

    to_right = [
        halo(vol_hbm.at[:, size_x - reach : size_x], vol_left, 0, right),
        halo(cot_hbm.at[:, deep_x - 1], cot_left, 1, right),
    ]
    to_left = [halo(vol_hbm.at[:, 0:reach], vol_right, 2, left), halo(cot_hbm.at[:, 0], cot_right, 3, left)]

    @pl.when(outer)
    def _():
        for copy in to_right:
            copy.start()

    @pl.when(inner)
    def _():
        for copy in to_left:
            copy.start()

    lane = lax.broadcasted_iota(jnp.int32, (1, 128), 1)
    deep_y = 2 * (lane & 1) + (lane >> 6)
    ro, co = grid_of(32, 128)
    loads[0].wait()
    t2 = dot(w2_ref[...].reshape(27 * 16, 32), pick(ro == (co & 63) >> 1))
    ro, co = grid_of(16, 128)
    loads[1].wait()
    w1 = jnp.concatenate([w1_ref[k].astype(f32) for k in range(27)], axis=0).astype(bf16)
    t1 = dot(w1, pick(ro == (co & 15)))
    ro, co = grid_of(8, 128)
    near_y = 2 * ((co & 63) >> 4) + (co >> 6)
    taps_y = [jnp.where(ro == near_y + q - 1, 1.0, 0.0) for q in range(3)]

    def tap2(k):
        return t2[16 * k : 16 * k + 16]

    w1_rows, w2_rows, wb_cols = [], [], []
    for p in range(3):
        for r in range(3):
            for c in range(4):
                rows = [4 * (9 * p + 3 * q + r) + c for q in range(3)]
                w1_rows.append(sum(t1[k : k + 1] * taps_y[q] for q, k in enumerate(rows)))
            ks = [9 * p + 3 * q + r for q in range(3)]
            block = []
            for y in range(4):
                w2_rows.append(sum(jnp.where(deep_y == y + 1 - q, tap2(k), 0.0) for q, k in enumerate(ks)))
                block.append(sum(jnp.where(deep_y == y + q - 1, tap2(26 - k), 0.0) for q, k in enumerate(ks)))
            wb_cols.append(jnp.concatenate(block, axis=0))
    w1_wide = jnp.concatenate(w1_rows, axis=0).T.astype(bf16)
    w2_wide = jnp.concatenate(w2_rows, axis=0).T.astype(bf16)
    wb_wide = jnp.concatenate(wb_cols, axis=1).astype(bf16)

    def taps_of(ref, i):
        return z_taps(ref[:, i].astype(f32).reshape(32, 128), 128)

    def first_cols(taps):
        count = len(taps) - 2
        return jnp.concatenate([jnp.concatenate(taps[p : p + count], axis=1) for p in range(3)], axis=0)

    loads[2].wait()
    taps_own = [taps_of(vol_ref, i) for i in range(size_x)]
    cols_mid = first_cols(taps_own)
    act_mid, slope_mid = activate_both(dot(w1_wide, cols_mid))
    act_mid = act_mid[:64] + act_mid[64:]

    ro, co = grid_of(256, 128)
    pool1[...] = pick((ro >> 7 == co >> 6) & ((ro & 127) >> 1 == (co & 63)), 0.125)
    ro, co = grid_of(384, 64)
    row = ro >> 6
    same = (row >= 1) & (row <= 4) & ((row - 1) >> 1 == co >> 5) & ((ro & 63) >> 1 == (co & 31))
    pool2[...] = pick(same, 0.125)
    ro, co = grid_of(128, 384)
    spread2[...] = pick((((co >> 6) + 1) >> 1 == ro >> 5) & ((co & 63) >> 1 == (ro & 31)), 0.125)
    ro, co = grid_of(128, 256)
    spread1[...] = pick((ro >> 6 == co >> 7) & ((ro & 63) == (co & 127) >> 1), 0.125)
    ro, co = grid_of(512, 128)
    gather2[...] = pick((ro >> 7 == co >> 5) & ((ro & 63) >> 1 == (co & 31)))
    ro, co = grid_of(384, 128)
    gather1[...] = pick((ro >> 7 == co >> 4) & ((ro & 15) == (co & 15)))

    loads[3].wait()

    @pl.when(outer)
    def _():
        for copy in to_right:
            copy.wait_send()
        for copy in to_left:
            copy.wait_recv()

    @pl.when(inner)
    def _():
        for copy in to_left:
            copy.wait_send()
        for copy in to_right:
            copy.wait_recv()

    taps_low = [taps_of(vol_left, i) for i in range(reach)] + taps_own[:2]
    taps_high = taps_own[-2:] + [taps_of(vol_right, i) for i in range(reach)]
    cols_low, cols_high = first_cols(taps_low), first_cols(taps_high)
    edge = 128 * (reach - 1)
    pre_low, pre_high = dot(w1_wide, cols_low), dot(w1_wide, cols_high)
    act_low, act_high = activate(pre_low[:, :edge]), activate(pre_high[:, 128:])
    act_first, slope_first = activate_both(pre_low[:, edge:])
    act_last, slope_last = activate_both(pre_high[:, :128])
    act1 = [act_low, act_first, None, act_last, act_high]
    act1 = [act_mid if x is None else x[:64] + x[64:] for x in act1]
    act1 = jnp.concatenate(act1, axis=1)
    slope1 = jnp.concatenate([slope_first, slope_mid, slope_last], axis=1)
    cols1 = jnp.concatenate([cols_low[:, edge:], cols_mid, cols_high[:, :128]], axis=1)
    pairs = []
    for j in range(4):
        four = [act1[:, 128 * (4 * j + i) : 128 * (4 * j + i + 1)] for i in range(4)]
        pairs.append(jnp.concatenate([four[0] + four[1], four[2] + four[3]], axis=1))
    acts = dot_wide(jnp.concatenate(pairs, axis=0), pool1[...]).astype(bf16).astype(f32)
    even = [acts[64 * j : 64 * j + 64] for j in range(4)]
    even[0] = jnp.where(inner, even[0], 0.0)
    even[3] = jnp.where(outer, even[3], 0.0)
    odd = [between(even[j], even[j + 1]) for j in range(3)]

    even_taps = [z_taps(x, 64) for x in even]
    odd_taps = [z_taps(x, 64) for x in odd]
    cols2 = jnp.concatenate(
        [jnp.concatenate([even_taps[j], odd_taps[j], even_taps[j + 1]], axis=0) for j in range(3)], axis=1
    )
    act2, slope2 = activate_both(dot(w2_wide, cols2))

    def cot_rows(values):
        return values.astype(f32).reshape(64, 32)

    cots = [cot_left[...], cot_ref[:, 0], cot_ref[:, 1], cot_right[...]]
    cots = jnp.concatenate([cot_rows(x) for x in cots], axis=1).astype(bf16)
    wide = dot(cots, spread2[...])
    delta2 = (slope2 * jnp.concatenate([wide, wide], axis=0)).astype(bf16).astype(f32)
    row = lax.broadcasted_iota(jnp.int32, (128, 384), 1) >> 6
    own2 = jnp.where((row >= 1) & (row <= 4), delta2, 0.0).astype(bf16)

    odd = [delta2[:, 128 * j : 128 * j + 128] for j in range(3)]
    odd_taps = [z_taps(x, 64) for x in odd]
    even_taps = [z_taps(between(odd[j], odd[j + 1]), 64) for j in range(2)]
    cols3 = jnp.concatenate(
        [jnp.concatenate([odd_taps[j], even_taps[j], odd_taps[j + 1]], axis=0) for j in range(2)], axis=1
    )
    back = dot(wb_wide, cols3).astype(bf16)
    wide = dot(jnp.concatenate([back[:, :128], back[:, 128:]], axis=0), spread1[...])
    rows = [wide[64 * (i // 2) : 64 * (i // 2) + 64, 128 * (i % 2) : 128 * (i % 2) + 128] for i in range(4)]
    wide = jnp.concatenate([rows[i // 2] for i in range(8)], axis=1)
    delta1 = (slope1 * jnp.concatenate([wide, wide], axis=0)).astype(bf16)

    grad2 = dot_lanes(cols2, own2)
    blocks = []
    for k in range(27):
        p, q, r = k // 9, k // 3 % 3, k % 3
        at = 64 * (3 * p + r)
        blocks.append(
            sum(jnp.where(deep_y == y + 1 - q, grad2[at + 16 * y : at + 16 * y + 16], 0.0) for y in range(4))
        )
    blocks.append(jnp.zeros((16, 128), f32))
    groups = [jnp.concatenate(blocks[7 * j : 7 * j + 7], axis=0) for j in range(4)]
    pay[0:112] = dot_wide(jnp.concatenate(groups, axis=1), gather2[...])

    grad1 = dot_lanes(cols1, delta1).reshape(36, 8, 128)
    groups = [jnp.sum(grad1 * taps_y[q][None], axis=1) for q in range(3)]
    groups = jnp.concatenate([jnp.concatenate(groups, axis=1), jnp.zeros((4, 384), f32)], axis=0)
    pay[112:152] = dot_wide(groups, gather1[...])
    if n_a * part > 152:
        pay[152:] = jnp.zeros((n_a * part - 152, 128), f32)

    def rows_of(t):
        return pl.ds(pl.multiple_of(t * part, 8), part)

    copies = []
    for step in range(1, n_a):
        t, to = in_a(step)
        i = step - 1
        copies.append(remote(pay.at[rows_of(t)], got.at[i], rs_send.at[i], rs_recv.at[i], to))
        copies[-1].start()
    feat_ref[...] = dot_wide(act2[:64] + act2[64:], pool2[...]).astype(bf16).astype(f32)
    total = pay[rows_of(a)]
    for i, copy in enumerate(copies):
        copy.wait_recv()
        total += got[i]

    across[b] = total
    others = []
    for step in range(1, n_b):
        i, to = step - 1, in_b(step)[1]
        others.append(remote(across.at[b], across.at[b], ex_send.at[i], ex_recv.at[i], to))
        others[-1].start()
    for copy in copies:
        copy.wait_send()
    for copy in others:
        copy.wait()
    total = across[0]
    for i in range(1, n_b):
        total += across[i]

    full[rows_of(a)] = total * (1.0 / n_dp)
    copies = []
    for step in range(1, n_a):
        i, to = step - 1, in_a(step)[1]
        copies.append(remote(full.at[rows_of(a)], full.at[rows_of(a)], ag_send.at[i], ag_recv.at[i], to))
        copies[-1].start()
    for copy in copies:
        copy.wait()
    sums_ref[...] = full[0:152]


def unpack(feat_ref, sums_ref, feat_hbm, g1_hbm, g2_hbm, feat_out, g1_out, g2_out, sems):
    for j in range(4):
        many = 7 if j < 3 else 6
        g2_out[7 * j : 7 * j + many] = sums_ref[0 : 16 * many, 32 * j : 32 * j + 32].reshape(many, 16, 32)
    copies = [pltpu.make_async_copy(g2_out, g2_hbm, sems.at[0])]
    copies[0].start()
    for i in range(2):
        feat_out[:, i] = feat_ref[:, 32 * i : 32 * i + 32].reshape(32, 2, 32).astype(bf16)
    copies.append(pltpu.make_async_copy(feat_out, feat_hbm, sems.at[1]))
    copies[1].start()
    for k in range(27):
        p, q, r = k // 9, k // 3 % 3, k % 3
        at = 112 + 4 * (3 * p + r)
        g1_out[k] = sums_ref[at : at + 4, 16 * q : 16 * q + 16]
    copies.append(pltpu.make_async_copy(g1_out, g1_hbm, sems.at[2]))
    copies[2].start()
    for copy in copies:
        copy.wait()


def shards(n_space, n_dp, volumes, first_kernel, middle_kernel, cotangent):
    n_a, n_b = 2 * n_space, n_dp // 2
    part = 8 * -(-152 // (8 * n_a))
    w1 = first_kernel.transpose(2, 3, 4, 1, 0).reshape(27, 4, 16)
    w2 = middle_kernel.transpose(2, 3, 4, 1, 0).reshape(27, 16, 32)
    cot = cotangent[0]
    vol = volumes[0]
    halo = (vol.shape[0], reach) + vol.shape[2:]
    edge = (cot.shape[0],) + cot.shape[2:]
    vmem = pl.BlockSpec(memory_space=pltpu.VMEM)
    hbm = pl.BlockSpec(memory_space=pltpu.HBM)
    dma = pltpu.SemaphoreType.DMA
    feat, sums = pl.pallas_call(
        functools.partial(kernel, n_space, n_dp, part),
        out_shape=(jax.ShapeDtypeStruct((64, 64), f32), jax.ShapeDtypeStruct((152, 128), f32)),
        in_specs=[hbm] * 4,
        out_specs=(vmem, vmem),
        scratch_shapes=[
            pltpu.VMEM(vol.shape, bf16),
            pltpu.VMEM(w1.shape, bf16),
            pltpu.VMEM(w2.shape, bf16),
            pltpu.VMEM(cot.shape, bf16),
            pltpu.VMEM(halo, bf16),
            pltpu.VMEM(halo, bf16),
            pltpu.VMEM(edge, bf16),
            pltpu.VMEM(edge, bf16),
            pltpu.VMEM((n_a * part, 128), f32),
            pltpu.VMEM((n_a - 1, part, 128), f32),
            pltpu.VMEM((n_b, part, 128), f32),
            pltpu.VMEM((n_a * part, 128), f32),
            pltpu.VMEM((256, 128), bf16),
            pltpu.VMEM((384, 64), bf16),
            pltpu.VMEM((128, 256), bf16),
            pltpu.VMEM((128, 384), bf16),
            pltpu.VMEM((384, 128), bf16),
            pltpu.VMEM((512, 128), bf16),
            dma((4,)),
            dma((4,)), dma((4,)),
            dma((n_a - 1,)), dma((n_a - 1,)),
            dma((max(n_b - 1, 1),)), dma((max(n_b - 1, 1),)),
            dma((n_a - 1,)), dma((n_a - 1,)),
        ],
        compiler_params=pltpu.CompilerParams(
            collective_id=0, has_side_effects=True, vmem_limit_bytes=48 * 1024 * 1024
        ),
        cost_estimate=pl.CostEstimate(flops=400_000_000, bytes_accessed=400_000, transcendentals=1_000_000),
    )(*[pltpu.with_memory_space_constraint(x, pltpu.HBM) for x in (vol, w1, w2, cot)])
    features, first_grad, middle_grad = pl.pallas_call(
        unpack,
        out_shape=(
            jax.ShapeDtypeStruct(cot.shape, bf16),
            jax.ShapeDtypeStruct((27, 4, 16), f32),
            jax.ShapeDtypeStruct((27, 16, 32), f32),
        ),
        in_specs=[vmem] * 2,
        out_specs=(hbm, hbm, hbm),
        scratch_shapes=[
            pltpu.VMEM(cot.shape, bf16),
            pltpu.VMEM((27, 4, 16), f32),
            pltpu.VMEM((27, 16, 32), f32),
            dma((3,)),
        ],
    )(feat, sums)
    first_grad = first_grad.reshape(3, 3, 3, 4, 16).transpose(4, 3, 0, 1, 2)
    middle_grad = middle_grad.reshape(3, 3, 3, 16, 32).transpose(4, 3, 0, 1, 2)
    return (features[None], first_grad, middle_grad)


def solution(mesh):
    in_specs = (P("dp", None, "space", None, None), P(), P(), P("dp", None, "space", None, None))
    out_specs = (P("dp", None, "space", None, None), P(), P())
    body = functools.partial(shards, mesh.shape["space"], mesh.shape["dp"])
    return jax.shard_map(body, mesh=mesh, in_specs=in_specs, out_specs=out_specs, check_vma=False)
```

time: 29 us -> 27 us (0.931)
  local copies, waits for them, and re-layouts: 4.51 us -> 1.22 us
  Pallas kernels: 23.6 us -> 24.9 us
    pallas_call x0 -> x1, Pallas kernels: none -> 1.74 us  [shards(): pl.pallas_call(unpack, out_shape=(jax.ShapeDtypeStruct(cot.shape, bf16),...]
    unnamed x8 -> x4, local copies, waits for them, and re-layouts: 2.89 us -> 1.22 us
    transpose x1 -> x0, local copies, waits for them, and re-layouts: 0.81 us -> none  [shards(): cot = cotangent[0].transpose(0, 2, 1, 3).reshape(64, 64)]
    reshape x3 -> x0, local copies, waits for them, and re-layouts: 0.81 us -> none  [the longest x2 0.72 us: shards(): features = feat.reshape(32, 2, 2, 32).transpose(0, 2, 1, 3)[None]]
    pallas_call x1, Pallas kernels: 23.6 us -> 23.2 us  [shards(): pl.pallas_call(functools.partial(kernel, n_space, n_dp, part), out_shape=...]
where the time goes in v1:
time: 27 us; the launch traced here: 26.8 us
  Pallas kernels  24.9 us (92%)
  local copies, waits for them, and re-layouts  1.22 us (5%)
  between operations  0.65 us (2%)
    pallas_call x1, Pallas kernels, shards(): pl.pallas_call(functools.partial(kernel, n_space, n_dp, part), out_shape=...  23.2 us
    pallas_call x1, Pallas kernels, shards(): pl.pallas_call(unpack, out_shape=(jax.ShapeDtypeStruct(cot.shape, bf16),...  1.74 us
    unnamed x4, local copies, waits for them, and re-layouts  1.22 us

profile of v1, /device:TPU:0, one launch (start us, length us, event | category | flops | bytes accessed | tf_op | source)
XLA Modules:
  0.0 26.8 jit_solution(4429392569654769933)
XLA Ops:
  0.6 23.2 %shard_map.67 = (f32[64,64]{1,0:T(8,128)S(1)}, f32[152,128]{1,0:T(8,128)S(1)}) custom-call(bf16[4,8,8,128]{3,2,1,0:T(8,128)(2,1)} %bitcast.17, bf16[27,4,16]{2,1,0:T(4,128)(2,1)} %bitcast.21, bf16[27,16,32]{2,1,0:T(8,128)(2,1)} %bitcast.16, bf16[32,2,2,32]{3,2,1,0:T(2,128)(2,1)} %bitcast.19), custom_call_target="tpu_custom_call" | custom-call | flops 400000000 | bytes 400000 | tf_op jit(solution)/shard_map/pallas_call | solution.py:356
  23.8 0.0 copy-start
  23.8 0.6 %copy-done = f32[152,128]{1,0:T(8,128)} copy-done((f32[152,128]{1,0:T(8,128)}, f32[152,128]{1,0:T(8,128)S(1)}, u32[]{:S(2)}) %copy-start) | copy-done | bytes 77848
  24.5 0.0 copy-start.1
  24.5 0.6 %copy-done.1 = f32[64,64]{1,0:T(8,128)} copy-done((f32[64,64]{1,0:T(8,128)}, f32[64,64]{1,0:T(8,128)S(1)}, u32[]{:S(2)}) %copy-start.1) | copy-done | bytes 16408
  25.1 1.7 %shard_map.68 = (bf16[32,2,2,32]{3,2,1,0:T(2,128)(2,1)}, f32[27,4,16]{2,1,0:T(4,128)}, f32[27,16,32]{2,1,0:T(8,128)}) custom-call(f32[64,64]{1,0:T(8,128)} %copy-done.1, f32[152,128]{1,0:T(8,128)} %copy-done), custom_call_target="tpu_custom_call" | custom-call | tf_op jit(solution)/shard_map/pallas_call | solution.py:391
Async XLA Ops:
  23.8 0.6 %copy-start = (f32[152,128]{1,0:T(8,128)}, f32[152,128]{1,0:T(8,128)S(1)}, u32[]{:S(2)}) copy-start(f32[152,128]{1,0:T(8,128)S(1)} %get-tuple-element.9.sums_ref) | copy-start | bytes 233476
  24.5 0.6 %copy-start.1 = (f32[64,64]{1,0:T(8,128)}, f32[64,64]{1,0:T(8,128)S(1)}, u32[]{:S(2)}) copy-start(f32[64,64]{1,0:T(8,128)S(1)} %get-tuple-element.8.feat_ref) | copy-start | bytes 49156

commit v2 on v1

--- a/solution.py
+++ b/solution.py
@@ -74,7 +74,7 @@
 def kernel(
     n_space, n_dp, part,
     vol_hbm, w1_hbm, w2_hbm, cot_hbm,
-    feat_ref, sums_ref,
+    out_ref,
     vol_ref, w1_ref, w2_ref, cot_ref, vol_left, vol_right, cot_left, cot_right, pay, got, across, full,
     pool1, pool2, spread1, spread2, gather1, gather2,
     load, halo_send, halo_recv, rs_send, rs_recv, ex_send, ex_recv, ag_send, ag_recv,
@@ -191,7 +191,7 @@
     spread1[...] = pick((ro >> 6 == co >> 7) & ((ro & 63) == (co & 127) >> 1), 0.125)
     ro, co = grid_of(512, 128)
     gather2[...] = pick((ro >> 7 == co >> 5) & ((ro & 63) >> 1 == (co & 31)))
-    ro, co = grid_of(384, 128)
+    ro, co = grid_of(896, 128)
     gather1[...] = pick((ro >> 7 == co >> 4) & ((ro & 15) == (co & 15)))
 
     loads[3].wait()
@@ -272,17 +272,18 @@
         )
     blocks.append(jnp.zeros((16, 128), f32))
     groups = [jnp.concatenate(blocks[7 * j : 7 * j + 7], axis=0) for j in range(4)]
-    pay[0:112] = dot_wide(jnp.concatenate(groups, axis=1), gather2[...])
+    pay[0:112] = dot(jnp.concatenate(groups, axis=1).astype(bf16), gather2[...]).astype(bf16)
 
     grad1 = dot_lanes(cols1, delta1).reshape(36, 8, 128)
-    groups = [jnp.sum(grad1 * taps_y[q][None], axis=1) for q in range(3)]
-    groups = jnp.concatenate([jnp.concatenate(groups, axis=1), jnp.zeros((4, 384), f32)], axis=0)
-    pay[112:152] = dot_wide(groups, gather1[...])
-    if n_a * part > 152:
-        pay[152:] = jnp.zeros((n_a * part - 152, 128), f32)
+    rows = [jnp.sum(grad1 * taps_y[q][None], axis=1) for q in range(3)]
+    rows = jnp.concatenate(rows + [jnp.zeros((4, 128), f32)], axis=0)
+    groups = jnp.concatenate([rows[16 * j : 16 * j + 16] for j in range(7)], axis=1)
+    pay[112:128] = dot(groups.astype(bf16), gather1[...]).astype(bf16)
+    if n_a * part > 128:
+        pay[128:] = jnp.zeros((n_a * part - 128, 128), bf16)
 
     def rows_of(t):
-        return pl.ds(pl.multiple_of(t * part, 8), part)
+        return pl.ds(pl.multiple_of(t * part, 16), part)
 
     copies = []
     for step in range(1, n_a):
@@ -290,13 +291,13 @@
         i = step - 1
         copies.append(remote(pay.at[rows_of(t)], got.at[i], rs_send.at[i], rs_recv.at[i], to))
         copies[-1].start()
-    feat_ref[...] = dot_wide(act2[:64] + act2[64:], pool2[...]).astype(bf16).astype(f32)
-    total = pay[rows_of(a)]
+    out_ref[128:192, 0:64] = dot_wide(act2[:64] + act2[64:], pool2[...]).astype(bf16).astype(f32)
+    total = pay[rows_of(a)].astype(f32)
     for i, copy in enumerate(copies):
         copy.wait_recv()
-        total += got[i]
-
-    across[b] = total
+        total += got[i].astype(f32)
+
+    across[b] = total.astype(bf16)
     others = []
     for step in range(1, n_b):
         i, to = step - 1, in_b(step)[1]
@@ -306,11 +307,11 @@
         copy.wait_send()
     for copy in others:
         copy.wait()
-    total = across[0]
+    total = across[0].astype(f32)
     for i in range(1, n_b):
-        total += across[i]
-
-    full[rows_of(a)] = total * (1.0 / n_dp)
+        total += across[i].astype(f32)
+
+    full[rows_of(a)] = (total * (1.0 / n_dp)).astype(bf16)
     copies = []
     for step in range(1, n_a):
         i, to = step - 1, in_a(step)[1]
@@ -318,23 +319,24 @@
         copies[-1].start()
     for copy in copies:
         copy.wait()
-    sums_ref[...] = full[0:152]
-
-
-def unpack(feat_ref, sums_ref, feat_hbm, g1_hbm, g2_hbm, feat_out, g1_out, g2_out, sems):
+    out_ref[0:128] = full[0:128].astype(f32)
+
+
+def unpack(in_ref, feat_hbm, g1_hbm, g2_hbm, feat_out, g1_out, g2_out, sems):
     for j in range(4):
         many = 7 if j < 3 else 6
-        g2_out[7 * j : 7 * j + many] = sums_ref[0 : 16 * many, 32 * j : 32 * j + 32].reshape(many, 16, 32)
+        g2_out[7 * j : 7 * j + many] = in_ref[0 : 16 * many, 32 * j : 32 * j + 32].reshape(many, 16, 32)
     copies = [pltpu.make_async_copy(g2_out, g2_hbm, sems.at[0])]
     copies[0].start()
     for i in range(2):
-        feat_out[:, i] = feat_ref[:, 32 * i : 32 * i + 32].reshape(32, 2, 32).astype(bf16)
+        feat_out[:, i] = in_ref[128:192, 32 * i : 32 * i + 32].reshape(32, 2, 32).astype(bf16)
     copies.append(pltpu.make_async_copy(feat_out, feat_hbm, sems.at[1]))
     copies[1].start()
     for k in range(27):
         p, q, r = k // 9, k // 3 % 3, k % 3
-        at = 112 + 4 * (3 * p + r)
-        g1_out[k] = sums_ref[at : at + 4, 16 * q : 16 * q + 16]
+        at = 36 * q + 4 * (3 * p + r)
+        row, col = 112 + at % 16, 16 * (at // 16)
+        g1_out[k] = in_ref[row : row + 4, col : col + 16]
     copies.append(pltpu.make_async_copy(g1_out, g1_hbm, sems.at[2]))
     copies[2].start()
     for copy in copies:
@@ -343,7 +345,7 @@
 
 def shards(n_space, n_dp, volumes, first_kernel, middle_kernel, cotangent):
     n_a, n_b = 2 * n_space, n_dp // 2
-    part = 8 * -(-152 // (8 * n_a))
+    part = 16 * -(-128 // (16 * n_a))
     w1 = first_kernel.transpose(2, 3, 4, 1, 0).reshape(27, 4, 16)
     w2 = middle_kernel.transpose(2, 3, 4, 1, 0).reshape(27, 16, 32)
     cot = cotangent[0]
@@ -353,11 +355,11 @@
     vmem = pl.BlockSpec(memory_space=pltpu.VMEM)
     hbm = pl.BlockSpec(memory_space=pltpu.HBM)
     dma = pltpu.SemaphoreType.DMA
-    feat, sums = pl.pallas_call(
+    packed = pl.pallas_call(
         functools.partial(kernel, n_space, n_dp, part),
-        out_shape=(jax.ShapeDtypeStruct((64, 64), f32), jax.ShapeDtypeStruct((152, 128), f32)),
+        out_shape=jax.ShapeDtypeStruct((192, 128), f32),
         in_specs=[hbm] * 4,
-        out_specs=(vmem, vmem),
+        out_specs=vmem,
         scratch_shapes=[
             pltpu.VMEM(vol.shape, bf16),
             pltpu.VMEM(w1.shape, bf16),
@@ -367,15 +369,15 @@
             pltpu.VMEM(halo, bf16),
             pltpu.VMEM(edge, bf16),
             pltpu.VMEM(edge, bf16),
-            pltpu.VMEM((n_a * part, 128), f32),
-            pltpu.VMEM((n_a - 1, part, 128), f32),
-            pltpu.VMEM((n_b, part, 128), f32),
-            pltpu.VMEM((n_a * part, 128), f32),
+            pltpu.VMEM((n_a * part, 128), bf16),
+            pltpu.VMEM((n_a - 1, part, 128), bf16),
+            pltpu.VMEM((n_b, part, 128), bf16),
+            pltpu.VMEM((n_a * part, 128), bf16),
             pltpu.VMEM((256, 128), bf16),
             pltpu.VMEM((384, 64), bf16),
             pltpu.VMEM((128, 256), bf16),
             pltpu.VMEM((128, 384), bf16),
-            pltpu.VMEM((384, 128), bf16),
+            pltpu.VMEM((896, 128), bf16),
             pltpu.VMEM((512, 128), bf16),
             dma((4,)),
             dma((4,)), dma((4,)),
@@ -384,7 +386,7 @@
             dma((n_a - 1,)), dma((n_a - 1,)),
         ],
         compiler_params=pltpu.CompilerParams(
-            collective_id=0, has_side_effects=True, vmem_limit_bytes=48 * 1024 * 1024
+            collective_id=0, has_side_effects=True, vmem_limit_bytes=24 * 1024 * 1024
         ),
         cost_estimate=pl.CostEstimate(flops=400_000_000, bytes_accessed=400_000, transcendentals=1_000_000),
     )(*[pltpu.with_memory_space_constraint(x, pltpu.HBM) for x in (vol, w1, w2, cot)])
@@ -395,7 +397,7 @@
             jax.ShapeDtypeStruct((27, 4, 16), f32),
             jax.ShapeDtypeStruct((27, 16, 32), f32),
         ),
-        in_specs=[vmem] * 2,
+        in_specs=[vmem],
         out_specs=(hbm, hbm, hbm),
         scratch_shapes=[
             pltpu.VMEM(cot.shape, bf16),
@@ -403,7 +405,8 @@
             pltpu.VMEM((27, 16, 32), f32),
             dma((3,)),
         ],
-    )(feat, sums)
+        compiler_params=pltpu.CompilerParams(vmem_limit_bytes=4 * 1024 * 1024),
+    )(packed)
     first_grad = first_grad.reshape(3, 3, 3, 4, 16).transpose(4, 3, 0, 1, 2)
     middle_grad = middle_grad.reshape(3, 3, 3, 16, 32).transpose(4, 3, 0, 1, 2)
     return (features[None], first_grad, middle_grad)

time: 27 us -> 24.1 us (0.89)
  Pallas kernels: 24.9 us -> 23.3 us
  local copies, waits for them, and re-layouts: 1.22 us -> 0 us
    unnamed x4 -> x0, local copies, waits for them, and re-layouts: 1.22 us -> none
    pallas_call x1, Pallas kernels: 1.74 us -> 0.84 us  [shards(): pl.pallas_call(unpack, out_shape=(jax.ShapeDtypeStruct(cot.shape, bf16),...]
    pallas_call x1, Pallas kernels: 23.2 us -> 22.5 us  [shards(): pl.pallas_call(functools.partial(kernel, n_space, n_dp, part), out_shape=...]
where the time goes in v2:
time: 24.1 us; the launch traced here: 24 us
  Pallas kernels  23.3 us (97%)
  between operations  0.64 us (3%)
    pallas_call x1, Pallas kernels, shards(): pl.pallas_call(functools.partial(kernel, n_space, n_dp, part), out_shape=...  22.5 us
    pallas_call x1, Pallas kernels, shards(): pl.pallas_call(unpack, out_shape=(jax.ShapeDtypeStruct(cot.shape, bf16),...  0.84 us

profile of v2, /device:TPU:0, one launch (start us, length us, event | category | flops | bytes accessed | tf_op | source)
XLA Modules:
  0.0 24.0 jit_solution(6265888832566900453)
XLA Ops:
  0.6 22.5 %shard_map.67.in_ref = f32[192,128]{1,0:T(8,128)S(1)} custom-call(bf16[4,8,8,128]{3,2,1,0:T(8,128)(2,1)} %bitcast.17, bf16[27,4,16]{2,1,0:T(4,128)(2,1)} %bitcast.21, bf16[27,16,32]{2,1,0:T(8,128)(2,1)} %bitcast.16, bf16[32,2,2,32]{3,2,1,0:T(2,128)(2,1)} %bitcast.19), custom_call_target="tpu_custom_call" | custom-call | flops 400000000 | bytes 400000 | tf_op jit(solution)/shard_map/pallas_call | solution.py:358
  23.1 0.8 %shard_map.68 = (bf16[32,2,2,32]{3,2,1,0:T(2,128)(2,1)}, f32[27,4,16]{2,1,0:T(4,128)}, f32[27,16,32]{2,1,0:T(8,128)}) custom-call(f32[192,128]{1,0:T(8,128)S(1)} %shard_map.67.in_ref), custom_call_target="tpu_custom_call" | custom-call | tf_op jit(solution)/shard_map/pallas_call | solution.py:393

commit v3 on v2

--- a/solution.py
+++ b/solution.py
@@ -250,6 +250,30 @@
     row = lax.broadcasted_iota(jnp.int32, (128, 384), 1) >> 6
     own2 = jnp.where((row >= 1) & (row <= 4), delta2, 0.0).astype(bf16)
 
+    grad2 = dot_lanes(cols2, own2)
+    blocks = []
+    for k in range(27):
+        p, q, r = k // 9, k // 3 % 3, k % 3
+        at = 64 * (3 * p + r)
+        blocks.append(
+            sum(jnp.where(deep_y == y + 1 - q, grad2[at + 16 * y : at + 16 * y + 16], 0.0) for y in range(4))
+        )
+    blocks.append(jnp.zeros((16, 128), f32))
+    groups = [jnp.concatenate(blocks[7 * j : 7 * j + 7], axis=0) for j in range(4)]
+    pay[0:112] = dot(jnp.concatenate(groups, axis=1).astype(bf16), gather2[...]).astype(bf16)
+    if n_a * part > 112:
+        pay[112:] = jnp.zeros((n_a * part - 112, 128), bf16)
+
+    def rows_of(t):
+        return pl.ds(pl.multiple_of(t * part, 16), part)
+
+    parts = []
+    for step in range(1, n_a):
+        t, to = in_a(step)
+        i = step - 1
+        parts.append(remote(pay.at[rows_of(t)], got.at[i], rs_send.at[i], rs_recv.at[i], to))
+        parts[-1].start()
+
     odd = [delta2[:, 128 * j : 128 * j + 128] for j in range(3)]
     odd_taps = [z_taps(x, 64) for x in odd]
     even_taps = [z_taps(between(odd[j], odd[j + 1]), 64) for j in range(2)]
@@ -262,48 +286,24 @@
     wide = jnp.concatenate([rows[i // 2] for i in range(8)], axis=1)
     delta1 = (slope1 * jnp.concatenate([wide, wide], axis=0)).astype(bf16)
 
-    grad2 = dot_lanes(cols2, own2)
-    blocks = []
-    for k in range(27):
-        p, q, r = k // 9, k // 3 % 3, k % 3
-        at = 64 * (3 * p + r)
-        blocks.append(
-            sum(jnp.where(deep_y == y + 1 - q, grad2[at + 16 * y : at + 16 * y + 16], 0.0) for y in range(4))
-        )
-    blocks.append(jnp.zeros((16, 128), f32))
-    groups = [jnp.concatenate(blocks[7 * j : 7 * j + 7], axis=0) for j in range(4)]
-    pay[0:112] = dot(jnp.concatenate(groups, axis=1).astype(bf16), gather2[...]).astype(bf16)
-
     grad1 = dot_lanes(cols1, delta1).reshape(36, 8, 128)
     rows = [jnp.sum(grad1 * taps_y[q][None], axis=1) for q in range(3)]
     rows = jnp.concatenate(rows + [jnp.zeros((4, 128), f32)], axis=0)
     groups = jnp.concatenate([rows[16 * j : 16 * j + 16] for j in range(7)], axis=1)
-    pay[112:128] = dot(groups.astype(bf16), gather1[...]).astype(bf16)
-    if n_a * part > 128:
-        pay[128:] = jnp.zeros((n_a * part - 128, 128), bf16)
-
-    def rows_of(t):
-        return pl.ds(pl.multiple_of(t * part, 16), part)
-
-    copies = []
-    for step in range(1, n_a):
-        t, to = in_a(step)
-        i = step - 1
-        copies.append(remote(pay.at[rows_of(t)], got.at[i], rs_send.at[i], rs_recv.at[i], to))
-        copies[-1].start()
-    out_ref[128:192, 0:64] = dot_wide(act2[:64] + act2[64:], pool2[...]).astype(bf16).astype(f32)
+    across[b, part:] = dot(groups.astype(bf16), gather1[...]).astype(bf16)
+
     total = pay[rows_of(a)].astype(f32)
-    for i, copy in enumerate(copies):
+    for i, copy in enumerate(parts):
         copy.wait_recv()
         total += got[i].astype(f32)
-
-    across[b] = total.astype(bf16)
+    across[b, :part] = total.astype(bf16)
     others = []
     for step in range(1, n_b):
         i, to = step - 1, in_b(step)[1]
         others.append(remote(across.at[b], across.at[b], ex_send.at[i], ex_recv.at[i], to))
         others[-1].start()
-    for copy in copies:
+    out_ref[128:192, 0:64] = dot_wide(act2[:64] + act2[64:], pool2[...]).astype(bf16).astype(f32)
+    for copy in parts:
         copy.wait_send()
     for copy in others:
         copy.wait()
@@ -311,15 +311,21 @@
     for i in range(1, n_b):
         total += across[i].astype(f32)
 
-    full[rows_of(a)] = (total * (1.0 / n_dp)).astype(bf16)
+    full[a] = (total * (1.0 / n_dp)).astype(bf16)
     copies = []
     for step in range(1, n_a):
         i, to = step - 1, in_a(step)[1]
-        copies.append(remote(full.at[rows_of(a)], full.at[rows_of(a)], ag_send.at[i], ag_recv.at[i], to))
+        copies.append(remote(full.at[a], full.at[a], ag_send.at[i], ag_recv.at[i], to))
         copies[-1].start()
     for copy in copies:
         copy.wait()
-    out_ref[0:128] = full[0:128].astype(f32)
+    for i in range(-(-112 // part)):
+        rows = min(part, 112 - part * i)
+        out_ref[part * i : part * i + rows] = full[i, :rows].astype(f32)
+    total = full[0, part:].astype(f32)
+    for i in range(1, n_a):
+        total += full[i, part:].astype(f32)
+    out_ref[112:128] = total
 
 
 def unpack(in_ref, feat_hbm, g1_hbm, g2_hbm, feat_out, g1_out, g2_out, sems):
@@ -345,7 +351,7 @@
 
 def shards(n_space, n_dp, volumes, first_kernel, middle_kernel, cotangent):
     n_a, n_b = 2 * n_space, n_dp // 2
-    part = 16 * -(-128 // (16 * n_a))
+    part = 16 * -(-112 // (16 * n_a))
     w1 = first_kernel.transpose(2, 3, 4, 1, 0).reshape(27, 4, 16)
     w2 = middle_kernel.transpose(2, 3, 4, 1, 0).reshape(27, 16, 32)
     cot = cotangent[0]
@@ -371,8 +377,8 @@
             pltpu.VMEM(edge, bf16),
             pltpu.VMEM((n_a * part, 128), bf16),
             pltpu.VMEM((n_a - 1, part, 128), bf16),
-            pltpu.VMEM((n_b, part, 128), bf16),
-            pltpu.VMEM((n_a * part, 128), bf16),
+            pltpu.VMEM((n_b, part + 16, 128), bf16),
+            pltpu.VMEM((n_a, part + 16, 128), bf16),
             pltpu.VMEM((256, 128), bf16),
             pltpu.VMEM((384, 64), bf16),
             pltpu.VMEM((128, 256), bf16),

time: 24.1 us -> 23.6 us (0.979)
  Pallas kernels: 23.3 us -> 22.8 us
    pallas_call x1, Pallas kernels: 22.5 us -> 22 us  [shards(): pl.pallas_call(functools.partial(kernel, n_space, n_dp, part), out_shape=...]
where the time goes in v3:
time: 23.6 us; the launch traced here: 23.5 us
  Pallas kernels  22.8 us (97%)
  between operations  0.64 us (3%)
    pallas_call x1, Pallas kernels, shards(): pl.pallas_call(functools.partial(kernel, n_space, n_dp, part), out_shape=...  22 us
    pallas_call x1, Pallas kernels, shards(): pl.pallas_call(unpack, out_shape=(jax.ShapeDtypeStruct(cot.shape, bf16),...  0.84 us

profile of v3, /device:TPU:0, one launch (start us, length us, event | category | flops | bytes accessed | tf_op | source)
XLA Modules:
  0.0 23.5 jit_solution(17094715591211136517)
XLA Ops:
  0.6 22.0 %shard_map.67.in_ref = f32[192,128]{1,0:T(8,128)S(1)} custom-call(bf16[4,8,8,128]{3,2,1,0:T(8,128)(2,1)} %bitcast.17, bf16[27,4,16]{2,1,0:T(4,128)(2,1)} %bitcast.21, bf16[27,16,32]{2,1,0:T(8,128)(2,1)} %bitcast.16, bf16[32,2,2,32]{3,2,1,0:T(2,128)(2,1)} %bitcast.19), custom_call_target="tpu_custom_call" | custom-call | flops 400000000 | bytes 400000 | tf_op jit(solution)/shard_map/pallas_call | solution.py:364
  22.6 0.8 %shard_map.68 = (bf16[32,2,2,32]{3,2,1,0:T(2,128)(2,1)}, f32[27,4,16]{2,1,0:T(4,128)}, f32[27,16,32]{2,1,0:T(8,128)}) custom-call(f32[192,128]{1,0:T(8,128)S(1)} %shard_map.67.in_ref), custom_call_target="tpu_custom_call" | custom-call | tf_op jit(solution)/shard_map/pallas_call | solution.py:399

commit v4 on v3

--- a/solution.py
+++ b/solution.py
@@ -3,6 +3,7 @@
 
 import jax
 import jax.numpy as jnp
+import numpy as np
 from jax import lax
 from jax.experimental import pallas as pl
 from jax.experimental.pallas import tpu as pltpu
@@ -15,17 +16,21 @@
 f32, bf16 = jnp.float32, jnp.bfloat16
 
 
-def activate(a):
-    soft = jnp.maximum(a, 0.0) + jnp.log(1.0 + jnp.exp(-jnp.abs(a)))
-    return leak_slope * a + soft_share * (soft - log_two)
-
-
-def activate_both(a):
-    small = jnp.exp(-jnp.abs(a))
-    whole = 1.0 + small
-    soft = jnp.maximum(a, 0.0) + jnp.log(whole)
-    act = leak_slope * a + soft_share * (soft - log_two)
-    return act, leak_slope + soft_share * (jnp.where(a >= 0.0, 1.0, small) / whole)
+def soft_terms(a):
+    return jnp.maximum(leak_slope * a, a), 1.0 + jnp.exp(-jnp.abs(a))
+
+
+def halves(terms):
+    x, y = terms
+    return x[:64] + x[64:], y[:64] * y[64:]
+
+
+def act_sum(x, y, count):
+    return x + soft_share * (jnp.log(y) - count * log_two)
+
+
+def slope_of(a):
+    return (leak_slope + 0.5 * soft_share) + 0.5 * soft_share * jnp.tanh(0.5 * a)
 
 
 def dot(a, b):
@@ -34,12 +39,6 @@
 
 def dot_lanes(a, b):
     return lax.dot_general(a, b, (((1,), (1,)), ((), ())), preferred_element_type=f32)
-
-
-def dot_wide(a, b):
-    high = a.astype(bf16)
-    low = (a - high.astype(f32)).astype(bf16)
-    return dot(high, b) + dot(low, b)
 
 
 def grid_of(rows, cols):
@@ -53,6 +52,25 @@
     return jnp.where(where, value, 0.0).astype(bf16)
 
 
+def tables():
+    def table(rows, cols, rule):
+        return rule(np.arange(rows)[:, None], np.arange(cols)[None, :])
+
+    pool1 = table(256, 128, lambda r, c: (r >> 7 == c >> 6) & ((r & 127) >> 1 == (c & 63))) * 0.125
+    row = (np.arange(384) >> 6)[:, None]
+    pool2 = table(384, 128, lambda r, c: ((r & 63) >> 1 == (c & 31)) & (c < 64) & ((row - 1) >> 1 == c >> 5))
+    pool2 = pool2 * 0.125 * ((row >= 1) & (row <= 4))
+    spread1 = table(128, 256, lambda r, c: (r >> 6 == c >> 7) & ((r & 63) == (c & 127) >> 1)) * 0.125
+    spread2 = table(128, 384, lambda r, c: (((c >> 6) + 1) >> 1 == r >> 5) & ((c & 63) >> 1 == (r & 31))) * 0.125
+    gather1 = table(896, 128, lambda r, c: (r >> 7 == c >> 4) & ((r & 15) == (c & 15)))
+    gather2 = table(512, 128, lambda r, c: (r >> 7 == c >> 5) & ((r & 63) >> 1 == (c & 31)))
+    parts = [pool1, pool2, *np.split(spread1, 2, 1), *np.split(spread2, 3, 1), gather1, gather2]
+    return np.concatenate(parts, 0).astype(np.float32).astype(bf16)
+
+
+at_pool1, at_pool2, at_spread1, at_spread2, at_gather1, at_gather2 = 0, 256, 640, 896, 1280, 2176
+
+
 def z_taps(a, width):
     place = lax.broadcasted_iota(jnp.int32, a.shape, 1) & (width - 1)
     before = jnp.where(place == 0, 0.0, pltpu.roll(a, 1, 1))
@@ -73,10 +91,10 @@
 
 def kernel(
     n_space, n_dp, part,
-    vol_hbm, w1_hbm, w2_hbm, cot_hbm,
+    vol_hbm, w1_hbm, w2_hbm, cot_hbm, table_hbm,
     out_ref,
     vol_ref, w1_ref, w2_ref, cot_ref, vol_left, vol_right, cot_left, cot_right, pay, got, across, full,
-    pool1, pool2, spread1, spread2, gather1, gather2,
+    table_ref,
     load, halo_send, halo_recv, rs_send, rs_recv, ex_send, ex_recv, ag_send, ag_recv,
 ):
     s, d = lax.axis_index("space"), lax.axis_index("dp")
@@ -96,7 +114,7 @@
     loads = [
         pltpu.make_async_copy(src, dst, load.at[i])
         for i, (src, dst) in enumerate(
-            [(w2_hbm, w2_ref), (w1_hbm, w1_ref), (vol_hbm, vol_ref), (cot_hbm, cot_ref)]
+            [(w2_hbm, w2_ref), (w1_hbm, w1_ref), (vol_hbm, vol_ref), (cot_hbm, cot_ref), (table_hbm, table_ref)]
         )
     ]
     for copy in loads:
@@ -176,25 +194,11 @@
     loads[2].wait()
     taps_own = [taps_of(vol_ref, i) for i in range(size_x)]
     cols_mid = first_cols(taps_own)
-    act_mid, slope_mid = activate_both(dot(w1_wide, cols_mid))
-    act_mid = act_mid[:64] + act_mid[64:]
-
-    ro, co = grid_of(256, 128)
-    pool1[...] = pick((ro >> 7 == co >> 6) & ((ro & 127) >> 1 == (co & 63)), 0.125)
-    ro, co = grid_of(384, 64)
-    row = ro >> 6
-    same = (row >= 1) & (row <= 4) & ((row - 1) >> 1 == co >> 5) & ((ro & 63) >> 1 == (co & 31))
-    pool2[...] = pick(same, 0.125)
-    ro, co = grid_of(128, 384)
-    spread2[...] = pick((((co >> 6) + 1) >> 1 == ro >> 5) & ((co & 63) >> 1 == (ro & 31)), 0.125)
-    ro, co = grid_of(128, 256)
-    spread1[...] = pick((ro >> 6 == co >> 7) & ((ro & 63) == (co & 127) >> 1), 0.125)
-    ro, co = grid_of(512, 128)
-    gather2[...] = pick((ro >> 7 == co >> 5) & ((ro & 63) >> 1 == (co & 31)))
-    ro, co = grid_of(896, 128)
-    gather1[...] = pick((ro >> 7 == co >> 4) & ((ro & 15) == (co & 15)))
+    pre_mid = dot(w1_wide, cols_mid)
+    sums_mid, slope_mid = halves(soft_terms(pre_mid)), slope_of(pre_mid)
 
     loads[3].wait()
+    loads[4].wait()
 
     @pl.when(outer)
     def _():
@@ -215,19 +219,20 @@
     cols_low, cols_high = first_cols(taps_low), first_cols(taps_high)
     edge = 128 * (reach - 1)
     pre_low, pre_high = dot(w1_wide, cols_low), dot(w1_wide, cols_high)
-    act_low, act_high = activate(pre_low[:, :edge]), activate(pre_high[:, 128:])
-    act_first, slope_first = activate_both(pre_low[:, edge:])
-    act_last, slope_last = activate_both(pre_high[:, :128])
-    act1 = [act_low, act_first, None, act_last, act_high]
-    act1 = [act_mid if x is None else x[:64] + x[64:] for x in act1]
-    act1 = jnp.concatenate(act1, axis=1)
-    slope1 = jnp.concatenate([slope_first, slope_mid, slope_last], axis=1)
+    sums = [halves(soft_terms(pre_low)), sums_mid, halves(soft_terms(pre_high))]
+    sum_x, sum_y = [jnp.concatenate(x, axis=1) for x in zip(*sums)]
+    slope1 = jnp.concatenate([slope_of(pre_low[:, edge:]), slope_mid, slope_of(pre_high[:, :128])], axis=1)
     cols1 = jnp.concatenate([cols_low[:, edge:], cols_mid, cols_high[:, :128]], axis=1)
     pairs = []
     for j in range(4):
-        four = [act1[:, 128 * (4 * j + i) : 128 * (4 * j + i + 1)] for i in range(4)]
-        pairs.append(jnp.concatenate([four[0] + four[1], four[2] + four[3]], axis=1))
-    acts = dot_wide(jnp.concatenate(pairs, axis=0), pool1[...]).astype(bf16).astype(f32)
+        pair = []
+        for at in (512 * j, 512 * j + 256):
+            x = sum_x[:, at : at + 128] + sum_x[:, at + 128 : at + 256]
+            y = sum_y[:, at : at + 128] * sum_y[:, at + 128 : at + 256]
+            pair.append(act_sum(x, y, 4))
+        pairs.append(jnp.concatenate(pair, axis=1))
+    pool = table_ref[at_pool1 : at_pool1 + 256]
+    acts = dot(jnp.concatenate(pairs, axis=0).astype(bf16), pool).astype(bf16).astype(f32)
     even = [acts[64 * j : 64 * j + 64] for j in range(4)]
     even[0] = jnp.where(inner, even[0], 0.0)
     even[3] = jnp.where(outer, even[3], 0.0)
@@ -238,14 +243,16 @@
     cols2 = jnp.concatenate(
         [jnp.concatenate([even_taps[j], odd_taps[j], even_taps[j + 1]], axis=0) for j in range(3)], axis=1
     )
-    act2, slope2 = activate_both(dot(w2_wide, cols2))
+    pre2 = dot(w2_wide, cols2)
+    slope2 = slope_of(pre2)
 
     def cot_rows(values):
         return values.astype(f32).reshape(64, 32)
 
     cots = [cot_left[...], cot_ref[:, 0], cot_ref[:, 1], cot_right[...]]
     cots = jnp.concatenate([cot_rows(x) for x in cots], axis=1).astype(bf16)
-    wide = dot(cots, spread2[...])
+    wide = [dot(cots, table_ref[at : at + 128]) for at in range(at_spread2, at_spread2 + 384, 128)]
+    wide = jnp.concatenate(wide, axis=1)
     delta2 = (slope2 * jnp.concatenate([wide, wide], axis=0)).astype(bf16).astype(f32)
     row = lax.broadcasted_iota(jnp.int32, (128, 384), 1) >> 6
     own2 = jnp.where((row >= 1) & (row <= 4), delta2, 0.0).astype(bf16)
@@ -260,7 +267,7 @@
         )
     blocks.append(jnp.zeros((16, 128), f32))
     groups = [jnp.concatenate(blocks[7 * j : 7 * j + 7], axis=0) for j in range(4)]
-    pay[0:112] = dot(jnp.concatenate(groups, axis=1).astype(bf16), gather2[...]).astype(bf16)
+    pay[0:112] = dot(jnp.concatenate(groups, axis=1).astype(bf16), table_ref[at_gather2 : at_gather2 + 512]).astype(bf16)
     if n_a * part > 112:
         pay[112:] = jnp.zeros((n_a * part - 112, 128), bf16)
 
@@ -281,7 +288,8 @@
         [jnp.concatenate([odd_taps[j], even_taps[j], odd_taps[j + 1]], axis=0) for j in range(2)], axis=1
     )
     back = dot(wb_wide, cols3).astype(bf16)
-    wide = dot(jnp.concatenate([back[:, :128], back[:, 128:]], axis=0), spread1[...])
+    spread = jnp.concatenate([table_ref[at : at + 128] for at in (at_spread1, at_spread1 + 128)], axis=1)
+    wide = dot(jnp.concatenate([back[:, :128], back[:, 128:]], axis=0), spread)
     rows = [wide[64 * (i // 2) : 64 * (i // 2) + 64, 128 * (i % 2) : 128 * (i % 2) + 128] for i in range(4)]
     wide = jnp.concatenate([rows[i // 2] for i in range(8)], axis=1)
     delta1 = (slope1 * jnp.concatenate([wide, wide], axis=0)).astype(bf16)
@@ -290,7 +298,7 @@
     rows = [jnp.sum(grad1 * taps_y[q][None], axis=1) for q in range(3)]
     rows = jnp.concatenate(rows + [jnp.zeros((4, 128), f32)], axis=0)
     groups = jnp.concatenate([rows[16 * j : 16 * j + 16] for j in range(7)], axis=1)
-    across[b, part:] = dot(groups.astype(bf16), gather1[...]).astype(bf16)
+    across[b, part:] = dot(groups.astype(bf16), table_ref[at_gather1 : at_gather1 + 896]).astype(bf16)
 
     total = pay[rows_of(a)].astype(f32)
     for i, copy in enumerate(parts):
@@ -302,7 +310,8 @@
         i, to = step - 1, in_b(step)[1]
         others.append(remote(across.at[b], across.at[b], ex_send.at[i], ex_recv.at[i], to))
         others[-1].start()
-    out_ref[128:192, 0:64] = dot_wide(act2[:64] + act2[64:], pool2[...]).astype(bf16).astype(f32)
+    act2 = act_sum(*halves(soft_terms(pre2)), 2).astype(bf16)
+    out_ref[128:192] = dot(act2, table_ref[at_pool2 : at_pool2 + 384]).astype(bf16).astype(f32)
     for copy in parts:
         copy.wait_send()
     for copy in others:
@@ -356,6 +365,7 @@
     w2 = middle_kernel.transpose(2, 3, 4, 1, 0).reshape(27, 16, 32)
     cot = cotangent[0]
     vol = volumes[0]
+    table = jnp.asarray(tables())
     halo = (vol.shape[0], reach) + vol.shape[2:]
     edge = (cot.shape[0],) + cot.shape[2:]
     vmem = pl.BlockSpec(memory_space=pltpu.VMEM)
@@ -364,7 +374,7 @@
     packed = pl.pallas_call(
         functools.partial(kernel, n_space, n_dp, part),
         out_shape=jax.ShapeDtypeStruct((192, 128), f32),
-        in_specs=[hbm] * 4,
+        in_specs=[hbm] * 5,
         out_specs=vmem,
         scratch_shapes=[
             pltpu.VMEM(vol.shape, bf16),
@@ -379,13 +389,8 @@
             pltpu.VMEM((n_a - 1, part, 128), bf16),
             pltpu.VMEM((n_b, part + 16, 128), bf16),
             pltpu.VMEM((n_a, part + 16, 128), bf16),
-            pltpu.VMEM((256, 128), bf16),
-            pltpu.VMEM((384, 64), bf16),
-            pltpu.VMEM((128, 256), bf16),
-            pltpu.VMEM((128, 384), bf16),
-            pltpu.VMEM((896, 128), bf16),
-            pltpu.VMEM((512, 128), bf16),
-            dma((4,)),
+            pltpu.VMEM(table.shape, bf16),
+            dma((5,)),
             dma((4,)), dma((4,)),
             dma((n_a - 1,)), dma((n_a - 1,)),
             dma((max(n_b - 1, 1),)), dma((max(n_b - 1, 1),)),
@@ -395,7 +400,7 @@
             collective_id=0, has_side_effects=True, vmem_limit_bytes=24 * 1024 * 1024
         ),
         cost_estimate=pl.CostEstimate(flops=400_000_000, bytes_accessed=400_000, transcendentals=1_000_000),
-    )(*[pltpu.with_memory_space_constraint(x, pltpu.HBM) for x in (vol, w1, w2, cot)])
+    )(*[pltpu.with_memory_space_constraint(x, pltpu.HBM) for x in (vol, w1, w2, cot, table)])
     features, first_grad, middle_grad = pl.pallas_call(
         unpack,
         out_shape=(

time: 23.6 us -> 23.4 us (level)
  no operation moved by 1% of the time
where the time goes in v4:
time: 23.4 us; the launch traced here: 23.3 us
  Pallas kernels  22.6 us (97%)
  between operations  0.64 us (3%)
    pallas_call x1, Pallas kernels, shards(): pl.pallas_call(functools.partial(kernel, n_space, n_dp, part), out_shape=...  21.8 us
    pallas_call x1, Pallas kernels, shards(): pl.pallas_call(unpack, out_shape=(jax.ShapeDtypeStruct(cot.shape, bf16),...  0.84 us

profile of v4, /device:TPU:0, one launch (start us, length us, event | category | flops | bytes accessed | tf_op | source)
XLA Modules:
  0.0 23.3 jit_solution(8196834671022715716)
XLA Ops:
  0.6 21.8 %shard_map.76.in_ref = f32[192,128]{1,0:T(8,128)S(1)} custom-call(bf16[4,8,8,128]{3,2,1,0:T(8,128)(2,1)} %bitcast.17, bf16[27,4,16]{2,1,0:T(4,128)(2,1)} %bitcast.21, bf16[27,16,32]{2,1,0:T(8,128)(2,1)} %bitcast.16, bf16[32,2,2,32]{3,2,1,0:T(2,128)(2,1)} %bitcast.19, bf16[2688,128]{1,0:T(8,128)(2,1)} %constant.2.clone.table_hbm), custom_call_target="tpu_custom_call" | custom-call | flops 400000000 | bytes 400000 | tf_op jit(solution)/shard_map/pallas_call | solution.py:374
  22.4 0.8 %shard_map.77 = (bf16[32,2,2,32]{3,2,1,0:T(2,128)(2,1)}, f32[27,4,16]{2,1,0:T(4,128)}, f32[27,16,32]{2,1,0:T(8,128)}) custom-call(f32[192,128]{1,0:T(8,128)S(1)} %shard_map.76.in_ref), custom_call_target="tpu_custom_call" | custom-call | tf_op jit(solution)/shard_map/pallas_call | solution.py:404

commit v5 on v4

--- a/solution.py
+++ b/solution.py
@@ -102,6 +102,7 @@
     a, b = 2 * s + lax.rem(d, 2), d // 2
     inner = s > 0
     outer = s < n_space - 1
+    size_x, deep_x = vol_hbm.shape[1], cot_hbm.shape[1]
 
     def in_a(step):
         t = lax.rem(a + step, n_a)
@@ -126,32 +127,6 @@
         pl.semaphore_signal(barrier, inc=1, device_id=in_a(step)[1], device_id_type=pl.DeviceIdType.MESH)
     for step in range(1, n_b):
         pl.semaphore_signal(barrier, inc=1, device_id=in_b(step)[1], device_id_type=pl.DeviceIdType.MESH)
-    pl.semaphore_wait(barrier, n_a - 1 + n_b - 1)
-
-    right = {"space": jnp.minimum(s + 1, n_space - 1), "dp": d}
-    left = {"space": jnp.maximum(s - 1, 0), "dp": d}
-    size_x = vol_hbm.shape[1]
-    deep_x = cot_hbm.shape[1]
-
-    def halo(src, dst, sem, to):
-        return remote(src, dst, halo_send.at[sem], halo_recv.at[sem], to)
-
-    to_right = [
-        halo(vol_hbm.at[:, size_x - reach : size_x], vol_left, 0, right),
-        halo(cot_hbm.at[:, deep_x - 1], cot_left, 1, right),
-    ]
-    to_left = [halo(vol_hbm.at[:, 0:reach], vol_right, 2, left), halo(cot_hbm.at[:, 0], cot_right, 3, left)]
-
-    @pl.when(outer)
-    def _():
-        for copy in to_right:
-            copy.start()
-
-    @pl.when(inner)
-    def _():
-        for copy in to_left:
-            copy.start()
-
     lane = lax.broadcasted_iota(jnp.int32, (1, 128), 1)
     deep_y = 2 * (lane & 1) + (lane >> 6)
     ro, co = grid_of(32, 128)
@@ -168,35 +143,65 @@
     def tap2(k):
         return t2[16 * k : 16 * k + 16]
 
-    w1_rows, w2_rows, wb_cols = [], [], []
+    w1_rows, w2_rows = [], []
     for p in range(3):
         for r in range(3):
             for c in range(4):
                 rows = [4 * (9 * p + 3 * q + r) + c for q in range(3)]
                 w1_rows.append(sum(t1[k : k + 1] * taps_y[q] for q, k in enumerate(rows)))
             ks = [9 * p + 3 * q + r for q in range(3)]
-            block = []
             for y in range(4):
                 w2_rows.append(sum(jnp.where(deep_y == y + 1 - q, tap2(k), 0.0) for q, k in enumerate(ks)))
-                block.append(sum(jnp.where(deep_y == y + q - 1, tap2(26 - k), 0.0) for q, k in enumerate(ks)))
-            wb_cols.append(jnp.concatenate(block, axis=0))
     w1_wide = jnp.concatenate(w1_rows, axis=0).T.astype(bf16)
     w2_wide = jnp.concatenate(w2_rows, axis=0).T.astype(bf16)
-    wb_wide = jnp.concatenate(wb_cols, axis=1).astype(bf16)
 
     def taps_of(ref, i):
         return z_taps(ref[:, i].astype(f32).reshape(32, 128), 128)
+
+    loads[2].wait()
+    taps_own = [taps_of(vol_ref, i) for i in range(size_x)]
+
+    pl.semaphore_wait(barrier, n_a - 1 + n_b - 1)
+
+    right = {"space": jnp.minimum(s + 1, n_space - 1), "dp": d}
+    left = {"space": jnp.maximum(s - 1, 0), "dp": d}
+
+    def halo(src, dst, sem, to):
+        return remote(src, dst, halo_send.at[sem], halo_recv.at[sem], to)
+
+    to_right = [
+        halo(vol_hbm.at[:, size_x - reach : size_x], vol_left, 0, right),
+        halo(cot_hbm, cot_left, 1, right),
+    ]
+    to_left = [halo(vol_hbm.at[:, 0:reach], vol_right, 2, left), halo(cot_hbm, cot_right, 3, left)]
+
+    @pl.when(outer)
+    def _():
+        for copy in to_right:
+            copy.start()
+
+    @pl.when(inner)
+    def _():
+        for copy in to_left:
+            copy.start()
 
     def first_cols(taps):
         count = len(taps) - 2
         return jnp.concatenate([jnp.concatenate(taps[p : p + count], axis=1) for p in range(3)], axis=0)
 
-    loads[2].wait()
-    taps_own = [taps_of(vol_ref, i) for i in range(size_x)]
     cols_mid = first_cols(taps_own)
     pre_mid = dot(w1_wide, cols_mid)
     sums_mid, slope_mid = halves(soft_terms(pre_mid)), slope_of(pre_mid)
 
+    wb_cols = []
+    for p in range(3):
+        for r in range(3):
+            ks = [26 - (9 * p + 3 * q + r) for q in range(3)]
+            block = [
+                sum(jnp.where(deep_y == y + q - 1, tap2(k), 0.0) for q, k in enumerate(ks)) for y in range(4)
+            ]
+            wb_cols.append(jnp.concatenate(block, axis=0))
+    wb_wide = jnp.concatenate(wb_cols, axis=1).astype(bf16)
     loads[3].wait()
     loads[4].wait()
 
@@ -249,7 +254,7 @@
     def cot_rows(values):
         return values.astype(f32).reshape(64, 32)
 
-    cots = [cot_left[...], cot_ref[:, 0], cot_ref[:, 1], cot_right[...]]
+    cots = [cot_left[:, deep_x - 1], cot_ref[:, 0], cot_ref[:, 1], cot_right[:, 0]]
     cots = jnp.concatenate([cot_rows(x) for x in cots], axis=1).astype(bf16)
     wide = [dot(cots, table_ref[at : at + 128]) for at in range(at_spread2, at_spread2 + 384, 128)]
     wide = jnp.concatenate(wide, axis=1)
@@ -367,7 +372,6 @@
     vol = volumes[0]
     table = jnp.asarray(tables())
     halo = (vol.shape[0], reach) + vol.shape[2:]
-    edge = (cot.shape[0],) + cot.shape[2:]
     vmem = pl.BlockSpec(memory_space=pltpu.VMEM)
     hbm = pl.BlockSpec(memory_space=pltpu.HBM)
     dma = pltpu.SemaphoreType.DMA
@@ -383,8 +387,8 @@
             pltpu.VMEM(cot.shape, bf16),
             pltpu.VMEM(halo, bf16),
             pltpu.VMEM(halo, bf16),
-            pltpu.VMEM(edge, bf16),
-            pltpu.VMEM(edge, bf16),
+            pltpu.VMEM(cot.shape, bf16),
+            pltpu.VMEM(cot.shape, bf16),
             pltpu.VMEM((n_a * part, 128), bf16),
             pltpu.VMEM((n_a - 1, part, 128), bf16),
             pltpu.VMEM((n_b, part + 16, 128), bf16),

time: 23.4 us -> 24.1 us (1.030)
  Pallas kernels: 22.6 us -> 23.3 us
    pallas_call x1, Pallas kernels: 21.8 us -> 22.5 us  [shards(): pl.pallas_call(functools.partial(kernel, n_space, n_dp, part), out_shape=...]
where the time goes in v5:
time: 24.1 us; the launch traced here: 24 us
  Pallas kernels  23.3 us (97%)
  between operations  0.64 us (3%)
    pallas_call x1, Pallas kernels, shards(): pl.pallas_call(functools.partial(kernel, n_space, n_dp, part), out_shape=...  22.5 us
    pallas_call x1, Pallas kernels, shards(): pl.pallas_call(unpack, out_shape=(jax.ShapeDtypeStruct(cot.shape, bf16),...  0.84 us

profile of v5, /device:TPU:0, one launch (start us, length us, event | category | flops | bytes accessed | tf_op | source)
XLA Modules:
  0.0 24.0 jit_solution(6702714864648466026)
XLA Ops:
  0.6 22.5 %shard_map.76.in_ref = f32[192,128]{1,0:T(8,128)S(1)} custom-call(bf16[4,8,8,128]{3,2,1,0:T(8,128)(2,1)} %bitcast.17, bf16[27,4,16]{2,1,0:T(4,128)(2,1)} %bitcast.21, bf16[27,16,32]{2,1,0:T(8,128)(2,1)} %bitcast.16, bf16[32,2,2,32]{3,2,1,0:T(2,128)(2,1)} %bitcast.19, bf16[2688,128]{1,0:T(8,128)(2,1)} %constant.2.clone.table_hbm), custom_call_target="tpu_custom_call" | custom-call | flops 400000000 | bytes 400000 | tf_op jit(solution)/shard_map/pallas_call | solution.py:378
  23.1 0.8 %shard_map.77 = (bf16[32,2,2,32]{3,2,1,0:T(2,128)(2,1)}, f32[27,4,16]{2,1,0:T(4,128)}, f32[27,16,32]{2,1,0:T(8,128)}) custom-call(f32[192,128]{1,0:T(8,128)S(1)} %shard_map.76.in_ref), custom_call_target="tpu_custom_call" | custom-call | tf_op jit(solution)/shard_map/pallas_call | solution.py:408

commit v6 on v4

--- a/solution.py
+++ b/solution.py
@@ -111,6 +111,11 @@
         t = lax.rem(b + step, n_b)
         return t, {"space": s, "dp": 2 * t + lax.rem(d, 2)}
 
+    barrier = pltpu.get_barrier_semaphore()
+    for step in sorted(range(1, n_a), key=lambda step: abs(min(step, n_a - step) - 2)):
+        pl.semaphore_signal(barrier, inc=1, device_id=in_a(step)[1], device_id_type=pl.DeviceIdType.MESH)
+    for step in range(1, n_b):
+        pl.semaphore_signal(barrier, inc=1, device_id=in_b(step)[1], device_id_type=pl.DeviceIdType.MESH)
     loads = [
         pltpu.make_async_copy(src, dst, load.at[i])
         for i, (src, dst) in enumerate(
@@ -119,13 +124,17 @@
     ]
     for copy in loads:
         copy.start()
-    for ref in (vol_left, vol_right, cot_left, cot_right):
-        ref[...] = jnp.zeros_like(ref)
-    barrier = pltpu.get_barrier_semaphore()
-    for step in range(1, n_a):
-        pl.semaphore_signal(barrier, inc=1, device_id=in_a(step)[1], device_id_type=pl.DeviceIdType.MESH)
-    for step in range(1, n_b):
-        pl.semaphore_signal(barrier, inc=1, device_id=in_b(step)[1], device_id_type=pl.DeviceIdType.MESH)
+
+    @pl.when(jnp.logical_not(inner))
+    def _():
+        vol_left[...] = jnp.zeros_like(vol_left)
+        cot_left[...] = jnp.zeros_like(cot_left)
+
+    @pl.when(jnp.logical_not(outer))
+    def _():
+        vol_right[...] = jnp.zeros_like(vol_right)
+        cot_right[...] = jnp.zeros_like(cot_right)
+
     pl.semaphore_wait(barrier, n_a - 1 + n_b - 1)
 
     right = {"space": jnp.minimum(s + 1, n_space - 1), "dp": d}
@@ -197,22 +206,18 @@
     pre_mid = dot(w1_wide, cols_mid)
     sums_mid, slope_mid = halves(soft_terms(pre_mid)), slope_of(pre_mid)
 
-    loads[3].wait()
-    loads[4].wait()
-
-    @pl.when(outer)
-    def _():
-        for copy in to_right:
-            copy.wait_send()
-        for copy in to_left:
-            copy.wait_recv()
-
-    @pl.when(inner)
-    def _():
-        for copy in to_left:
-            copy.wait_send()
-        for copy in to_right:
-            copy.wait_recv()
+    def halo_wait(i):
+        @pl.when(outer)
+        def _():
+            to_right[i].wait_send()
+            to_left[i].wait_recv()
+
+        @pl.when(inner)
+        def _():
+            to_left[i].wait_send()
+            to_right[i].wait_recv()
+
+    halo_wait(0)
 
     taps_low = [taps_of(vol_left, i) for i in range(reach)] + taps_own[:2]
     taps_high = taps_own[-2:] + [taps_of(vol_right, i) for i in range(reach)]
@@ -231,6 +236,7 @@
             y = sum_y[:, at : at + 128] * sum_y[:, at + 128 : at + 256]
             pair.append(act_sum(x, y, 4))
         pairs.append(jnp.concatenate(pair, axis=1))
+    loads[4].wait()
     pool = table_ref[at_pool1 : at_pool1 + 256]
     acts = dot(jnp.concatenate(pairs, axis=0).astype(bf16), pool).astype(bf16).astype(f32)
     even = [acts[64 * j : 64 * j + 64] for j in range(4)]
@@ -249,6 +255,8 @@
     def cot_rows(values):
         return values.astype(f32).reshape(64, 32)
 
+    loads[3].wait()
+    halo_wait(1)
     cots = [cot_left[...], cot_ref[:, 0], cot_ref[:, 1], cot_right[...]]
     cots = jnp.concatenate([cot_rows(x) for x in cots], axis=1).astype(bf16)
     wide = [dot(cots, table_ref[at : at + 128]) for at in range(at_spread2, at_spread2 + 384, 128)]

time: 23.4 us -> 23.5 us (level)
  no operation moved by 1% of the time
where the time goes in v6:
time: 23.5 us; the launch traced here: 23.4 us
  Pallas kernels  22.7 us (97%)
  between operations  0.64 us (3%)
    pallas_call x1, Pallas kernels, shards(): pl.pallas_call(functools.partial(kernel, n_space, n_dp, part), out_shape=...  21.9 us
    pallas_call x1, Pallas kernels, shards(): pl.pallas_call(unpack, out_shape=(jax.ShapeDtypeStruct(cot.shape, bf16),...  0.84 us

profile of v6, /device:TPU:0, one launch (start us, length us, event | category | flops | bytes accessed | tf_op | source)
XLA Modules:
  0.0 23.4 jit_solution(16745772400730791096)
XLA Ops:
  0.6 21.9 %shard_map.76.in_ref = f32[192,128]{1,0:T(8,128)S(1)} custom-call(bf16[4,8,8,128]{3,2,1,0:T(8,128)(2,1)} %bitcast.17, bf16[27,4,16]{2,1,0:T(4,128)(2,1)} %bitcast.21, bf16[27,16,32]{2,1,0:T(8,128)(2,1)} %bitcast.16, bf16[32,2,2,32]{3,2,1,0:T(2,128)(2,1)} %bitcast.19, bf16[2688,128]{1,0:T(8,128)(2,1)} %constant.2.clone.table_hbm), custom_call_target="tpu_custom_call" | custom-call | flops 400000000 | bytes 400000 | tf_op jit(solution)/shard_map/pallas_call | solution.py:382
  22.5 0.8 %shard_map.77 = (bf16[32,2,2,32]{3,2,1,0:T(2,128)(2,1)}, f32[27,4,16]{2,1,0:T(4,128)}, f32[27,16,32]{2,1,0:T(8,128)}) custom-call(f32[192,128]{1,0:T(8,128)S(1)} %shard_map.76.in_ref), custom_call_target="tpu_custom_call" | custom-call | tf_op jit(solution)/shard_map/pallas_call | solution.py:412

commit v7 on v4

--- a/solution.py
+++ b/solution.py
@@ -117,7 +117,7 @@
             [(w2_hbm, w2_ref), (w1_hbm, w1_ref), (vol_hbm, vol_ref), (cot_hbm, cot_ref), (table_hbm, table_ref)]
         )
     ]
-    for copy in loads:
+    for copy in loads[:4]:
         copy.start()
     for ref in (vol_left, vol_right, cot_left, cot_right):
         ref[...] = jnp.zeros_like(ref)
@@ -151,6 +151,8 @@
     def _():
         for copy in to_left:
             copy.start()
+
+    loads[4].start()
 
     lane = lax.broadcasted_iota(jnp.int32, (1, 128), 1)
     deep_y = 2 * (lane & 1) + (lane >> 6)

time: 23.4 us -> 23.4 us (level)
  no operation moved by 1% of the time
where the time goes in v7:
time: 23.4 us; the launch traced here: 23.3 us
  Pallas kernels  22.6 us (97%)
  between operations  0.64 us (3%)
    pallas_call x1, Pallas kernels, shards(): pl.pallas_call(functools.partial(kernel, n_space, n_dp, part), out_shape=...  21.8 us
    pallas_call x1, Pallas kernels, shards(): pl.pallas_call(unpack, out_shape=(jax.ShapeDtypeStruct(cot.shape, bf16),...  0.84 us

profile of v7, /device:TPU:0, one launch (start us, length us, event | category | flops | bytes accessed | tf_op | source)
XLA Modules:
  0.0 23.3 jit_solution(9048034416033825249)
XLA Ops:
  0.6 21.8 %shard_map.76.in_ref = f32[192,128]{1,0:T(8,128)S(1)} custom-call(bf16[4,8,8,128]{3,2,1,0:T(8,128)(2,1)} %bitcast.17, bf16[27,4,16]{2,1,0:T(4,128)(2,1)} %bitcast.21, bf16[27,16,32]{2,1,0:T(8,128)(2,1)} %bitcast.16, bf16[32,2,2,32]{3,2,1,0:T(2,128)(2,1)} %bitcast.19, bf16[2688,128]{1,0:T(8,128)(2,1)} %constant.2.clone.table_hbm), custom_call_target="tpu_custom_call" | custom-call | flops 400000000 | bytes 400000 | tf_op jit(solution)/shard_map/pallas_call | solution.py:376
  22.4 0.8 %shard_map.77 = (bf16[32,2,2,32]{3,2,1,0:T(2,128)(2,1)}, f32[27,4,16]{2,1,0:T(4,128)}, f32[27,16,32]{2,1,0:T(8,128)}) custom-call(f32[192,128]{1,0:T(8,128)S(1)} %shard_map.76.in_ref), custom_call_target="tpu_custom_call" | custom-call | tf_op jit(solution)/shard_map/pallas_call | solution.py:406
